TPU v7x, 512 devices: a whole 4x8x8 slice. The times are simulated.
512 devices in a mesh: seq: 32 (over z, x_hi, core), head: 16 (over y, x_lo).
Axes of the slice: x: 4 (x_hi: 2, x_lo: 2; x = x_hi * 2 + x_lo), y: 8, z: 8, core: 2. Of those that a mesh axis runs over, the one named last changes fastest.
Arguments:
- q_payload: bfloat16 [4096, 6144], P(('seq', 'head')), may hold values from -5 to 5
- k_payload: bfloat16 [4096, 6144], P(('seq', 'head')), may hold values from -4 to 4
- v_payload: bfloat16 [4096, 6144], P(('seq', 'head')), may hold values from -5 to 5
- exponents: int32 [3, 4096, 48], P(None, ('seq', 'head')), may hold values from -1 to 1
- lengths: int32 [4], replicated, may hold values from 1 to 3072, as said below
Outputs:
- attended: bfloat16 [4096, 6144], P(('seq', 'head'))
Inputs may be any that keep to these rules, and one draw needn't show every extreme that they name: `lengths`: 4 counts of at least 1 that sum to 4096; the largest is exactly 3072.
All inputs are finite; a program needn't handle non-finite values.
Results may differ from a plain program's by a relative error of at most 0.0045.
Values may be sent and summed in bfloat16 or wider, within the bound.
No kernel may reach another device: no remote copies, remote signals or barrier semaphores. Data moves between devices by JAX's collectives and lax.ppermute only.
A program may use at most 64 MiB of HBM per device.

v0:
```python
import math

import jax
import jax.numpy as jnp
from jax import lax
from jax.sharding import PartitionSpec as P


def dequantize(payload, exps, head_count, head_size):
    tok_rows = payload.shape[0]
    scaling = jnp.exp2(exps.astype(jnp.float32))
    shaped = payload.astype(jnp.float32).reshape(tok_rows, head_count, head_size)
    return (
        (shaped * scaling[:, :, None])
        .astype(jnp.bfloat16)
        .reshape(tok_rows, head_count * head_size)
    )


def clip_index(clip_ends, positions):
    return jnp.sum((clip_ends[None, :] <= positions[:, None]).astype(jnp.int32), axis=1)


def body(q_payload, k_payload, v_payload, exponents, lengths):
    head_count = exponents.shape[2]
    head_size = q_payload.shape[1] // head_count
    query = dequantize(q_payload, exponents[0], head_count, head_size)
    keyset = dequantize(k_payload, exponents[1], head_count, head_size)
    valset = dequantize(v_payload, exponents[2], head_count, head_size)
    query, keyset, valset = (
        lax.all_to_all(query, "head", split_axis=1, concat_axis=0, tiled=True),
        lax.all_to_all(keyset, "head", split_axis=1, concat_axis=0, tiled=True),
        lax.all_to_all(valset, "head", split_axis=1, concat_axis=0, tiled=True),
    )
    query_rows, local_width = query.shape
    local_heads = local_width // head_size
    inverse = 1.0 / math.sqrt(head_size)
    clip_ends = jnp.cumsum(lengths)
    block_first = lax.axis_index("seq") * query_rows
    query_clip = clip_index(clip_ends, block_first + jnp.arange(query_rows, dtype=jnp.int32))
    query_heads = query.reshape(query_rows, local_heads, head_size)
    initial = (
        jnp.full((local_heads, query_rows), -1e30, jnp.float32),
        jnp.zeros((local_heads, query_rows), jnp.float32),
        jnp.zeros((local_heads, query_rows, head_size), jnp.float32),
    )
    running = initial
    first_row = jnp.int32(0)
    key_part = lax.all_gather(keyset, "seq", axis=0, tiled=True)
    val_part = lax.all_gather(valset, "seq", axis=0, tiled=True)
    part_rows = key_part.shape[0]
    width_rows = min(part_rows, 1024)
    for lower in range(0, part_rows, width_rows):
        upper = min(lower + width_rows, part_rows)
        key_key_part = key_part[lower:upper]
        key_val_part = val_part[lower:upper]
        key_first_row = first_row + lower
        key_run_max, key_run_sum, key_run_acc = running
        key_part_rows = key_key_part.shape[0]
        key_clip = clip_index(clip_ends, key_first_row + jnp.arange(key_part_rows, dtype=jnp.int32))
        key_heads = key_key_part.reshape(key_part_rows, local_heads, head_size)
        val_heads = key_val_part.reshape(key_part_rows, local_heads, head_size)
        scores = (
            jnp.einsum("qhd,khd->hqk", query_heads, key_heads, preferred_element_type=jnp.float32)
            * inverse
        )
        keep = (query_clip[:, None] == key_clip[None, :])[None, :, :]
        scores = jnp.where(keep, scores, -1e30)
        new_max = jnp.maximum(key_run_max, jnp.max(scores, axis=2))
        factor = jnp.exp(key_run_max - new_max)
        weights = jnp.where(keep, jnp.exp(scores - new_max[:, :, None]), 0.0)
        new_sum = key_run_sum * factor + jnp.sum(weights, axis=2)
        added = jnp.einsum(
            "hqk,khd->hqd",
            weights.astype(jnp.bfloat16),
            val_heads,
            preferred_element_type=jnp.float32,
        )
        running = (new_max, new_sum, key_run_acc * factor[:, :, None] + added)
    run_max, run_sum, run_acc = running
    result = (run_acc / run_sum[:, :, None]).astype(jnp.bfloat16)
    result = jnp.transpose(result, (1, 0, 2)).reshape(query_rows, local_width)
    return lax.all_to_all(result, "head", split_axis=0, concat_axis=1, tiled=True)


def solution(mesh):
    return jax.shard_map(
        body,
        mesh=mesh,
        in_specs=(
            P(("seq", "head"), None),
            P(("seq", "head"), None),
            P(("seq", "head"), None),
            P(None, ("seq", "head"), None),
            P(),
        ),
        out_specs=P(("seq", "head"), None),
        check_vma=False,
    )
```

profile of v0, /device:TPU:1, one launch (start us, length us, event | category | flops | bytes accessed | tf_op | source)
XLA Modules:
  0.0 249.0 jit_solution(13930852191835128344)
XLA Ops:
  6.5 0.0 copy-start.7
  6.5 0.0 all-gather.3.cloned.1.call-start
  6.5 0.7 exponential_bitcast_fusion.2
  7.3 0.1 copy.52
  7.4 1.0 fusion.34
  8.4 16.8 %all_to_all.73 = bf16[8,16,384]{2,0,1:T(8,128)(2,1)} all-to-all(bf16[8,16,384]{2,0,1:T(8,128)(2,1)S(1)} %bitcast.151), channel_id=1, replica_groups=mesh['seq'=32,'head'=16] {'head'}, dimensions={1} | all-to-all | bytes 196608 | tf_op jit(solution)/shard_map/all_to_all | solution.py:32
  25.2 0.0 all-gather.3.cloned.1.call-update
  25.2 0.0 all-gather.5.cloned.1.call-start
  25.2 0.1 copy.56
  25.3 1.0 fusion.33
  26.3 11.6 %all_to_all.74 = bf16[8,16,384]{2,0,1:T(8,128)(2,1)} all-to-all(bf16[8,16,384]{2,0,1:T(8,128)(2,1)S(1)} %bitcast.152), channel_id=1, replica_groups=mesh['seq'=32,'head'=16] {'head'}, dimensions={1} | all-to-all | bytes 196608 | tf_op jit(solution)/shard_map/all_to_all | solution.py:33
  37.9 0.0 all-gather.5.cloned.1.call-update
  37.9 0.1 copy.51
  38.0 1.7 fusion.35
  39.6 3.5 %all-to-all-start = ((bf16[8,16,384]{2,0,1:T(8,128)(2,1)}), bf16[8,16,384]{2,0,1:T(8,128)(2,1)S(1)}, u32[]{:S(2)}, u32[]{:S(2)}) async-start(bf16[8,16,384]{2,0,1:T(8,128)(2,1)} %bitcast.4), calls=%async_computation | async-start | bytes 196608 | tf_op jit(solution)/shard_map/all_to_all | solution.py:31
  43.2 0.0 copy-done.7
  43.2 0.2 reduce-window.8
  43.4 0.1 convert_reduce_fusion.4
  43.4 0.1 convert_reduce_fusion
  43.6 1.1 broadcast_compare_fusion.1
  44.6 6.8 %all-to-all-done = bf16[8,16,384]{2,0,1:T(8,128)(2,1)S(1)} async-done(((bf16[8,16,384]{2,0,1:T(8,128)(2,1)}), bf16[8,16,384]{2,0,1:T(8,128)(2,1)S(1)}, u32[]{:S(2)}, u32[]{:S(2)}) %all-to-all-start) | async-done | bytes 98336 | tf_op jit(solution)/shard_map/all_to_all | solution.py:31
  51.4 64.7 %all-gather.3.cloned.1.call-done = bf16[4096,384]{1,0:T(8,128)(2,1)} async-done(((bf16[128,384]{1,0:T(8,128)(2,1)}), bf16[4096,384]{1,0:T(8,128)(2,1)}) %all-gather.3.cloned.1.call-update) | async-done | bytes 3145744 | tf_op jit(solution)/shard_map/all_gather | solution.py:49
  116.1 2.2 fusion.56
  118.3 1.2 copy.64
  119.5 85.9 %all-gather.5.cloned.1.call-done = bf16[4096,384]{1,0:T(8,128)(2,1)} async-done(((bf16[128,384]{1,0:T(8,128)(2,1)}), bf16[4096,384]{1,0:T(8,128)(2,1)}) %all-gather.5.cloned.1.call-update) | async-done | bytes 3145744 | tf_op jit(solution)/shard_map/all_gather | solution.py:50
  205.4 3.3 %fusion.55 = (bf16[1024,384]{1,0:T(8,128)(2,1)}, bf16[1024,384]{1,0:T(8,128)(2,1)}, bf16[1024,384]{1,0:T(8,128)(2,1)}, bf16[1024,384]{1,0:T(8,128)(2,1)S(1)}) fusion(bf16[4096,384]{1,0:T(8,128)(2,1)} %all-gather.5.cloned.1.call-done), kind=kLoop, calls=%fused_computation.92 | loop fusion | bytes 6291456 | tf_op jit(solution)/shard_map/slice | solution.py:56
  208.7 2.3 copy.72
  211.0 2.3 copy.67
  213.3 2.3 copy.62
  215.6 1.2 copy.57
  216.8 0.3 copy.69
  217.1 0.3 copy.59
  217.4 0.3 copy.53
  217.7 0.0 copy-start.1
  217.7 1.5 fusion.60
  219.2 0.0 copy-done.1
  219.2 0.5 fusion.59
  219.7 0.0 copy-start
  219.7 0.5 fusion.57
  220.3 0.6 copy-done
  220.9 0.5 fusion.58
  221.4 0.5 fusion.6
  221.9 0.0 copy-start.2
  221.9 0.5 fusion.4
  222.4 0.0 copy-start.6
  222.4 0.5 fusion.2
  222.9 0.0 copy-done.2
  222.9 0.5 fusion
  223.4 0.0 copy-start.5
  223.5 0.1 copy-done.6
  223.6 0.5 fusion.15
  224.1 0.0 copy-start.4
  224.1 0.5 copy-done.5
  224.6 0.5 fusion.13
  225.1 0.0 copy-start.3
  225.1 0.2 copy-done.4
  225.3 0.5 fusion.11
  225.8 0.5 copy-done.3
  226.3 0.5 fusion.16
  226.8 0.1 copy.74
  226.9 0.1 all_to_all.65
  227.0 14.5 %all_to_all.75 = bf16[16,8,384]{2,1,0:T(8,128)(2,1)S(1)} all-to-all(bf16[16,8,384]{2,1,0:T(8,128)(2,1)S(1)} %all_to_all.65), channel_id=1, replica_groups=mesh['seq'=32,'head'=16] {'head'}, dimensions={0} | all-to-all | bytes 196608 | tf_op jit(solution)/shard_map/all_to_all | solution.py:83
  241.6 0.6 copy.100
  (6 shorter events, 0.1 us)
Async XLA Ops:
  6.5 36.6 %copy-start.7 = (s32[4]{0:T(128)S(1)}, s32[4]{0:T(128)}, u32[]{:S(2)}) copy-start(s32[4]{0:T(128)} %param.9) | copy-start | bytes 52
  6.5 109.6 %all-gather.3.cloned.1.call-start = ((), (), s32[]{:S(2)}) async-start(), calls=%async_computation.4 | async-start | bytes 3244032 | tf_op jit(solution)/shard_map/all_gather | solution.py:49
  25.2 180.2 %all-gather.5.cloned.1.call-start = ((), (), s32[]{:S(2)}) async-start(), calls=%async_computation.5 | async-start | bytes 3244032 | tf_op jit(solution)/shard_map/all_gather | solution.py:50
  39.6 11.8 %all-to-all-start = ((bf16[8,16,384]{2,0,1:T(8,128)(2,1)}), bf16[8,16,384]{2,0,1:T(8,128)(2,1)S(1)}, u32[]{:S(2)}, u32[]{:S(2)}) async-start(bf16[8,16,384]{2,0,1:T(8,128)(2,1)} %bitcast.4), calls=%async_computation | async-start | bytes 196608 | tf_op jit(solution)/shard_map/all_to_all | solution.py:31
  217.7 1.5 copy-start.1
  219.7 1.1 copy-start
  221.9 1.0 copy-start.2
  222.4 1.2 copy-start.6
  223.4 1.2 copy-start.5
  224.1 1.2 copy-start.4
  225.1 1.2 copy-start.3
Sparse Core Ops, SparseCore 0:
  25.3 90.7 all-gather.2
  119.5 85.8 all-gather.4
where the time goes:
time: 250 us; the launch traced here: 249 us
  waiting for transfers between devices  157 us (63%)
  blocking collectives  42.9 us (17%)
  local copies, waits for them, and re-layouts  18.6 us (7%)
  between operations  13.6 us (5%)
  other arithmetic  7.9 us (3%)
  matrix products  5.17 us (2%)
  starting transfers between devices  3.55 us (1%)
    all_gather x1, waiting for transfers between devices, body(): val_part = lax.all_gather(valset, 'seq', axis=0, tiled=True)  85.9 us
    all_gather x1, waiting for transfers between devices, body(): key_part = lax.all_gather(keyset, 'seq', axis=0, tiled=True)  64.7 us
    all_to_all x1, blocking collectives, body(): lax.all_to_all(keyset, 'head', split_axis=1, concat_axis=0, tiled=True)  16.8 us
    all_to_all x1, blocking collectives, body(): lax.all_to_all(result, 'head', split_axis=0, concat_axis=1, tiled=True)  14.5 us
    all_to_all x1, blocking collectives, body(): lax.all_to_all(valset, 'head', split_axis=1, concat_axis=0, tiled=True)  11.6 us
    slice x5, local copies, waits for them, and re-layouts, body(): key_val_part = val_part[lower:upper]  11.4 us
    all_to_all x1, waiting for transfers between devices, body(): lax.all_to_all(query, 'head', split_axis=1, concat_axis=0, tiled=True)  6.77 us
  transfers between devices with their start and end apart: 3, of which 3 were waited for; matrix products, arithmetic and copies ran while one was open for 3% of the time, Pallas kernels for 0%

commit v1 on v0

v1 whole, which is shorter than its diff:
```python
import functools
import math

import jax
import jax.numpy as jnp
from jax import lax
from jax.experimental import pallas as pl
from jax.experimental.pallas import tpu as pltpu
from jax.sharding import Mesh
from jax.sharding import PartitionSpec as P

AXES = ("z", "xh", "core", "y", "xl")
SIZES = (8, 2, 2, 8, 2)
SLOTS = 64
HEADS = 48
HEAD = 128
ROWS = 8
OWN = SLOTS * ROWS
X = ("xh", "xl")


def pack_kernel(q_ref, k_ref, v_ref, e_ref, out_ref):
    scale = jnp.exp2(e_ref[...].astype(jnp.float32))
    for place, ref in enumerate((k_ref, v_ref, q_ref)):
        kind = (1, 2, 0)[place]
        for head in range(HEADS):
            part = ref[:, head * HEAD : (head + 1) * HEAD].astype(jnp.float32)
            out_ref[head, place * ROWS : (place + 1) * ROWS, :] = (
                part * scale[kind, :, head : head + 1]
            ).astype(jnp.bfloat16)
    out_ref[HEADS:, :, :] = jnp.zeros((SLOTS - HEADS, 3 * ROWS, HEAD), jnp.bfloat16)


def clip_of(length_ref, token):
    end = jnp.int32(0)
    clip = jnp.zeros_like(token)
    for i in range(4):
        end = end + length_ref[i]
        clip = clip + (end <= token).astype(jnp.int32)
    return clip


def token_of(row, xh, core, xl):
    z = row // 64
    y = (row // 8) % 8
    return z * 512 + xh * 256 + core * 128 + y * 16 + xl * 8 + row % 8


QB = 128


def attend_kernel(length_ref, q_ref, near_ref, far_ref, out_ref, s_ref):
    xh, xl, core = lax.axis_index("xh"), lax.axis_index("xl"), lax.axis_index("core")
    factor = math.log2(math.e) / math.sqrt(HEAD)
    key_row = lax.broadcasted_iota(jnp.int32, (1, OWN), 1)
    key_clip = []
    blocks = []
    for ref, its_core in ((near_ref, core), (far_ref, 1 - core)):
        for x in range(4):
            key_clip.append(clip_of(length_ref, token_of(key_row, x // 2, its_core, x % 2)))
            blocks.append((ref, x))
    for first in range(0, OWN, QB):
        query_row = first + lax.broadcasted_iota(jnp.int32, (QB, 1), 0)
        query_clip = clip_of(length_ref, token_of(query_row, xh, core, xl))
        query = q_ref[first : first + QB, :]
        top = jnp.full((QB, HEAD), -1e30, jnp.float32)
        for i, (ref, x) in enumerate(blocks):
            scores = lax.dot_general(
                query, ref[x, 0], (((1,), (1,)), ((), ())), preferred_element_type=jnp.float32
            )
            scores = jnp.where(query_clip == key_clip[i], scores, -1e30)
            s_ref[:, i * OWN : (i + 1) * OWN] = scores
            for j in range(0, OWN, HEAD):
                top = jnp.maximum(top, scores[:, j : j + HEAD])
        top = jnp.max(top, axis=1, keepdims=True) * factor
        total = jnp.zeros((QB, HEAD), jnp.float32)
        numerator = jnp.zeros((QB, HEAD), jnp.float32)
        for i, (ref, x) in enumerate(blocks):
            weights = jnp.exp2(s_ref[:, i * OWN : (i + 1) * OWN] * factor - top)
            for j in range(0, OWN, HEAD):
                total = total + weights[:, j : j + HEAD]
            numerator = numerator + jnp.dot(
                weights.astype(jnp.bfloat16), ref[x, 1], preferred_element_type=jnp.float32
            )
        total = jnp.sum(total, axis=1, keepdims=True)
        out_ref[first : first + QB, :] = (numerator / total).astype(jnp.bfloat16)


def unpack_kernel(in_ref, out_ref):
    for head in range(HEADS):
        out_ref[:, head * HEAD : (head + 1) * HEAD] = in_ref[head]


VMEM = pl.BlockSpec(memory_space=pltpu.VMEM)
SMEM = pl.BlockSpec(memory_space=pltpu.SMEM)


def body(q_payload, k_payload, v_payload, exponents, lengths):
    packed = pl.pallas_call(
        pack_kernel,
        out_shape=jax.ShapeDtypeStruct((SLOTS, 3 * ROWS, HEAD), jnp.bfloat16),
        in_specs=[VMEM] * 4,
        out_specs=VMEM,
    )(q_payload, k_payload, v_payload, exponents)
    mine = lax.all_to_all(packed, ("z", "y"), 0, 0, tiled=True)
    keys = mine[:, :ROWS].reshape(1, OWN, HEAD)
    values = mine[:, ROWS : 2 * ROWS].reshape(1, OWN, HEAD)
    query = mine[:, 2 * ROWS :].reshape(OWN, HEAD)
    own = jnp.concatenate([keys, values], axis=0)[None]
    near = lax.all_to_all(jnp.broadcast_to(own, (4, 2, OWN, HEAD)), X, 0, 0, tiled=True)
    far = lax.ppermute(near, "core", [(0, 1), (1, 0)])
    attended = pl.pallas_call(
        attend_kernel,
        out_shape=jax.ShapeDtypeStruct((OWN, HEAD), jnp.bfloat16),
        in_specs=[SMEM, VMEM, VMEM, VMEM],
        out_specs=VMEM,
        scratch_shapes=[pltpu.VMEM((QB, 8 * OWN), jnp.float32)],
        compiler_params=pltpu.CompilerParams(vmem_limit_bytes=40 * 2**20),
    )(lengths, query, near, far)
    back = lax.all_to_all(attended.reshape(SLOTS, ROWS, HEAD), ("z", "y"), 0, 0, tiled=True)
    return pl.pallas_call(
        unpack_kernel,
        out_shape=jax.ShapeDtypeStruct((ROWS, HEADS * HEAD), jnp.bfloat16),
        in_specs=[VMEM],
        out_specs=VMEM,
    )(back)


def solution(mesh):
    fine = Mesh(mesh.devices.reshape(SIZES), AXES)
    tokens = P(AXES, None)
    return jax.shard_map(
        body,
        mesh=fine,
        in_specs=(tokens, tokens, tokens, P(None, AXES, None), P()),
        out_specs=tokens,
        check_vma=False,
    )
```

time: 250 us -> 82.9 us (0.33)
  waiting for transfers between devices: 157 us -> 2.26 us
  blocking collectives: 42.9 us -> 64.7 us
  local copies, waits for them, and re-layouts: 18.6 us -> 0.21 us
  between operations: 13.6 us -> 0.04 us
  Pallas kernels: 0 us -> 8.57 us
  other arithmetic: 7.9 us -> 0.03 us
  matrix products: 5.17 us -> 0 us
  starting transfers between devices: 3.55 us -> 6.78 us
    all_gather x2 -> x0, waiting for transfers between devices: 151 us -> none  [the longest x1 85.9 us: body(): val_part = lax.all_gather(valset, 'seq', axis=0, tiled=True)]
    all_to_all x3, blocking collectives: 42.9 us -> 64.7 us  [the longest x1 32.2 us: body(): mine = lax.all_to_all(packed, ('z', 'y'), 0, 0, tiled=True)]
    slice x10 -> x0, local copies, waits for them, and re-layouts: 15.6 us -> none  [the longest x5 11.4 us: body(): key_val_part = val_part[lower:upper]]
    pallas_call x0 -> x3, Pallas kernels: none -> 8.57 us  [the longest x1 4.95 us: body(): pl.pallas_call(attend_kernel, out_shape=jax.ShapeDtypeStruct((OWN, HEAD),...]
    ppermute x0 -> x1, starting transfers between devices: none -> 6.78 us  [body(): far = lax.ppermute(near, 'core', [(0, 1), (1, 0)])]
    all_to_all x1 -> x0, waiting for transfers between devices: 6.77 us -> none  [body(): lax.all_to_all(query, 'head', split_axis=1, concat_axis=0, tiled=True)]
    dot_general x8 -> x0, matrix products: 5.17 us -> none  [the longest x4 3.07 us: body(): jnp.einsum('qhd,khd->hqk', query_heads, key_heads, preferred_element_type...]
    convert_element_type x3 -> x0, other arithmetic: 3.67 us -> none  [dequantize(): return (shaped * scaling[:, :, None]).astype(jnp.bfloat16).reshape(tok_ro...]
  transfers between devices with their start and end apart: 3 -> 1, of which waited for: 3 -> 1; matrix products, arithmetic and copies ran while one was open for 3% -> 0% of each run, Pallas kernels for 0% -> 0%
where the time goes in v1:
time: 82.9 us; the launch traced here: 82.6 us
  blocking collectives  64.7 us (78%)
  Pallas kernels  8.57 us (10%)
  starting transfers between devices  6.78 us (8%)
  waiting for transfers between devices  2.26 us (3%)
    all_to_all x1, blocking collectives, body(): mine = lax.all_to_all(packed, ('z', 'y'), 0, 0, tiled=True)  32.2 us
    all_to_all x1, blocking collectives, body(): lax.all_to_all(attended.reshape(SLOTS, ROWS, HEAD), ('z', 'y'), 0, 0, til...  17.5 us
    all_to_all x1, blocking collectives, body(): lax.all_to_all(jnp.broadcast_to(own, (4, 2, OWN, HEAD)), X, 0, 0, tiled=T...  15.1 us
    ppermute x1, starting transfers between devices, body(): far = lax.ppermute(near, 'core', [(0, 1), (1, 0)])  6.78 us
    pallas_call x1, Pallas kernels, body(): pl.pallas_call(attend_kernel, out_shape=jax.ShapeDtypeStruct((OWN, HEAD),...  4.95 us
    ppermute x1, waiting for transfers between devices, body(): far = lax.ppermute(near, 'core', [(0, 1), (1, 0)])  2.26 us
    pallas_call x1, Pallas kernels, body(): pl.pallas_call(pack_kernel, out_shape=jax.ShapeDtypeStruct((SLOTS, 3 * RO...  2.07 us
  transfers between devices with their start and end apart: 1, of which 1 were waited for; matrix products, arithmetic and copies ran while one was open for 0% of the time, Pallas kernels for 0%

profile of v1, /device:TPU:1, one launch (start us, length us, event | category | flops | bytes accessed | tf_op | source)
XLA Modules:
  0.0 82.6 jit_solution(15375806620177674883)
XLA Ops:
  0.0 2.1 %shard_map.55 = bf16[64,24,128]{2,1,0:T(8,128)(2,1)} custom-call(bf16[8,6144]{1,0:T(8,128)(2,1)} %q_ref.1, bf16[8,6144]{1,0:T(8,128)(2,1)} %k_ref.1, bf16[8,6144]{1,0:T(8,128)(2,1)} %v_ref.1, s32[3,8,48]{2,1,0:T(8,128)} %e_ref.1), custom_call_target="tpu_custom_call" | custom-call | tf_op jit(solution)/shard_map/pallas_call | solution.py:99
  2.1 32.2 %all_to_all.15 = bf16[64,24,128]{2,1,0:T(8,128)(2,1)S(1)} all-to-all(bf16[64,24,128]{2,1,0:T(8,128)(2,1)} %shard_map.55), channel_id=1, replica_groups=mesh['z'=8,'xh'=2,'core'=2,'y'=8,'xl'=2] {'z','y'}, dimensions={0} | all-to-all | bytes 786432 | tf_op jit(solution)/shard_map/all_to_all | solution.py:105
  34.2 0.1 slice_bitcast_fusion.1
  34.3 0.1 broadcast_in_dim.2
  34.5 15.1 %all_to_all.16.near_ref = bf16[4,2,512,128]{3,2,1,0:T(8,128)(2,1)S(1)} all-to-all(bf16[4,2,512,128]{3,2,1,0:T(8,128)(2,1)S(1)} %broadcast_in_dim.2), channel_id=1, replica_groups=mesh['z'=8,'xh'=2,'core'=2,'y'=8,'xl'=2] {'xh','xl'}, dimensions={0} | all-to-all | bytes 2097152 | tf_op jit(solution)/shard_map/all_to_all | solution.py:110
  49.6 0.0 copy-start
  49.6 6.8 %collective-permute-start = (bf16[4,2,512,128]{3,2,1,0:T(8,128)(2,1)S(1)}, bf16[4,2,512,128]{3,2,1,0:T(8,128)(2,1)S(1)}, u32[]{:S(2)}, u32[]{:S(2)}) collective-permute-start(bf16[4,2,512,128]{3,2,1,0:T(8,128)(2,1)S(1)} %all_to_all.16.near_ref), channel_id=1, source_target_pairs={{0,16},{16,0},{1,17},{17,1},{2,18},{18,2},{3,19},{19,3},{4,20},{20... | collective-permute-start | bytes 3145736 | tf_op jit(solution)/shard_map/ppermute | solution.py:111
  56.4 2.3 %collective-permute-done.far_ref = bf16[4,2,512,128]{3,2,1,0:T(8,128)(2,1)S(1)} collective-permute-done((bf16[4,2,512,128]{3,2,1,0:T(8,128)(2,1)S(1)}, bf16[4,2,512,128]{3,2,1,0:T(8,128)(2,1)S(1)}, u32[]{:S(2)}, u32[]{:S(2)}) %collective-permute-start) | collective-permute-done | bytes 1048608 | tf_op jit(solution)/shard_map/ppermute | solution.py:111
  58.6 0.0 copy-done
  58.7 4.9 %shard_map.56 = bf16[512,128]{1,0:T(8,128)(2,1)S(1)} custom-call(s32[4]{0:T(128)S(1)} %copy-done, bf16[512,128]{1,0:T(8,128)(2,1)S(1)} %get-tuple-element.7.q_ref, bf16[4,2,512,128]{3,2,1,0:T(8,128)(2,1)S(1)} %all_to_all.16.near_ref, bf16[4,2,512,128]{3,2,1,0:T(8,128)(2,1)S(1)} %collective-permute-done.far_ref), custom_call_target="tpu_custom_call" | custom-call | tf_op jit(solution)/shard_map/pallas_call | solution.py:112
  63.6 17.5 %all_to_all.17.in_ref = bf16[64,8,128]{2,1,0:T(8,128)(2,1)} all-to-all(bf16[64,8,128]{2,1,0:T(8,128)(2,1)S(1)} %bitcast.7), channel_id=1, replica_groups=mesh['z'=8,'xh'=2,'core'=2,'y'=8,'xl'=2] {'z','y'}, dimensions={0} | all-to-all | bytes 262144 | tf_op jit(solution)/shard_map/all_to_all | solution.py:120
  81.1 1.6 %shard_map.57 = bf16[8,6144]{1,0:T(8,128)(2,1)} custom-call(bf16[64,8,128]{2,1,0:T(8,128)(2,1)} %all_to_all.17.in_ref), custom_call_target="tpu_custom_call" | custom-call | tf_op jit(solution)/shard_map/pallas_call | solution.py:121
  (1 shorter events, 0.0 us)
Async XLA Ops:
  49.6 9.1 %copy-start = (s32[4]{0:T(128)S(1)}, s32[4]{0:T(128)}, u32[]{:S(2)}) copy-start(s32[4]{0:T(128)} %length_ref.1) | copy-start | bytes 52
  49.6 9.1 %collective-permute-start = (bf16[4,2,512,128]{3,2,1,0:T(8,128)(2,1)S(1)}, bf16[4,2,512,128]{3,2,1,0:T(8,128)(2,1)S(1)}, u32[]{:S(2)}, u32[]{:S(2)}) collective-permute-start(bf16[4,2,512,128]{3,2,1,0:T(8,128)(2,1)S(1)} %all_to_all.16.near_ref), channel_id=1, source_target_pairs={{0,16},{16,0},{1,17},{17,1},{2,18},{18,2},{3,19},{19,3},{4,20},{20... | collective-permute-start | bytes 3145736 | tf_op jit(solution)/shard_map/ppermute | solution.py:111

commit v2 on v1

v2 whole, which is shorter than its diff:
```python
import functools
import math

import jax
import jax.numpy as jnp
from jax import lax
from jax.experimental import pallas as pl
from jax.experimental.pallas import tpu as pltpu
from jax.sharding import Mesh
from jax.sharding import PartitionSpec as P

AXES = ("z", "xh", "core", "y", "xl")
SIZES = (8, 2, 2, 8, 2)
SLOTS = 64
HEADS = 48
HEAD = 128
ROWS = 8
OWN = SLOTS * ROWS
X = ("xh", "xl")


def clip_of(length_ref, token):
    end = jnp.int32(0)
    clip = jnp.zeros_like(token)
    for i in range(4):
        end = end + length_ref[i]
        clip = clip + (end <= token).astype(jnp.int32)
    return clip


def token_of(row, xh, core, xl):
    z = row // 64
    y = (row // 8) % 8
    return z * 512 + xh * 256 + core * 128 + y * 16 + xl * 8 + row % 8


QB = 256


def attend_kernel(its_core, carried, length_ref, q_ref, kv_ref, *refs):
    if carried:
        acc_ref, top_ref, sum_ref, out_ref, s_ref = refs
    else:
        acc_ref, top_ref, sum_ref, s_ref = refs
    xh, xl, core = lax.axis_index("xh"), lax.axis_index("xl"), lax.axis_index("core")
    key_core = core if its_core else 1 - core
    factor = math.log2(math.e) / math.sqrt(HEAD)
    key_row = lax.broadcasted_iota(jnp.int32, (1, OWN), 1)
    key_clip = [
        clip_of(length_ref, token_of(key_row, x // 2, key_core, x % 2)) for x in range(4)
    ]
    blocks = OWN // QB

    def rows(block):
        return slice(block * QB, (block + 1) * QB)

    def begin(block):
        query_row = block * QB + lax.broadcasted_iota(jnp.int32, (QB, 1), 0)
        query_clip = clip_of(length_ref, token_of(query_row, xh, core, xl))
        top = top_ref[rows(block), :] if carried else jnp.full((QB, HEAD), -1e30, jnp.float32)
        return q_ref[rows(block), :], query_clip, top

    def score(block, x, query, query_clip, top):
        scores = lax.dot_general(
            query, kv_ref[x, 0], (((1,), (1,)), ((), ())), preferred_element_type=jnp.float32
        )
        scores = jnp.where(query_clip == key_clip[x], scores, -1e30)
        s_ref[block % 2, :, x * OWN : (x + 1) * OWN] = scores
        for j in range(0, OWN, HEAD):
            top = jnp.maximum(top, scores[:, j : j + HEAD])
        return top

    query, query_clip, top = begin(0)
    for x in range(4):
        top = score(0, x, query, query_clip, top)
    for block in range(blocks):
        highest = jnp.max(top, axis=1, keepdims=True)
        shift = highest * factor
        if carried:
            old = jnp.exp2(top_ref[rows(block), :] * factor - shift)
            total, numerator = sum_ref[rows(block), :] * old, acc_ref[rows(block), :] * old
        else:
            total = numerator = jnp.zeros((QB, HEAD), jnp.float32)
        if block + 1 < blocks:
            query, query_clip, top = begin(block + 1)
        for x in range(4):
            if block + 1 < blocks:
                top = score(block + 1, x, query, query_clip, top)
            weights = jnp.exp2(s_ref[block % 2, :, x * OWN : (x + 1) * OWN] * factor - shift)
            for j in range(0, OWN, HEAD):
                total = total + weights[:, j : j + HEAD]
            numerator = numerator + jnp.dot(
                weights.astype(jnp.bfloat16), kv_ref[x, 1], preferred_element_type=jnp.float32
            )
        if carried:
            out_ref[rows(block), :] = (
                numerator / jnp.sum(total, axis=1, keepdims=True)
            ).astype(jnp.bfloat16)
        else:
            acc_ref[rows(block), :] = numerator
            top_ref[rows(block), :] = jnp.broadcast_to(highest, (QB, HEAD))
            sum_ref[rows(block), :] = total


VMEM = pl.BlockSpec(memory_space=pltpu.VMEM)
SMEM = pl.BlockSpec(memory_space=pltpu.SMEM)


def attend(its_core, lengths, query, kv, state=()):
    f32 = jax.ShapeDtypeStruct((OWN, HEAD), jnp.float32)
    return pl.pallas_call(
        functools.partial(attend_kernel, its_core, bool(state)),
        out_shape=jax.ShapeDtypeStruct((OWN, HEAD), jnp.bfloat16) if state else [f32] * 3,
        in_specs=[SMEM] + [VMEM] * (2 + len(state)),
        out_specs=VMEM if state else [VMEM] * 3,
        scratch_shapes=[pltpu.VMEM((2, QB, 4 * OWN), jnp.float32)],
        compiler_params=pltpu.CompilerParams(vmem_limit_bytes=32 * 2**20),
        cost_estimate=pl.CostEstimate(
            flops=4 * OWN * 4 * OWN * HEAD, bytes_accessed=2**20, transcendentals=4 * OWN * OWN
        ),
    )(lengths, query, kv, *state)


def pack(q_payload, k_payload, v_payload, exponents):
    scale = jnp.exp2(exponents.astype(jnp.float32))
    payload = jnp.stack([q_payload, k_payload, v_payload]).reshape(3, ROWS, HEADS, HEAD)
    scaled = (payload.astype(jnp.float32) * scale[:, :, :, None]).astype(jnp.bfloat16)
    packed = scaled.transpose(2, 0, 1, 3).reshape(HEADS, 3 * ROWS, HEAD)
    return jnp.pad(packed, ((0, SLOTS - HEADS), (0, 0), (0, 0)))


def body(q_payload, k_payload, v_payload, exponents, lengths):
    packed = pack(q_payload, k_payload, v_payload, exponents)
    mine = lax.all_to_all(packed, ("z", "y"), 0, 0, tiled=True)
    query = mine[:, :ROWS].reshape(OWN, HEAD)
    own = mine[:, ROWS:].reshape(1, SLOTS, 2, ROWS, HEAD).transpose(0, 2, 1, 3, 4)
    own = own.reshape(1, 2, OWN, HEAD)
    near = lax.all_to_all(jnp.broadcast_to(own, (4, 2, OWN, HEAD)), X, 0, 0, tiled=True)
    far = lax.ppermute(near, "core", [(0, 1), (1, 0)])
    state = attend(True, lengths, query, near)
    attended = attend(False, lengths, query, far, state)
    back = lax.all_to_all(attended.reshape(SLOTS, ROWS, HEAD), ("z", "y"), 0, 0, tiled=True)
    return back[:HEADS].transpose(1, 0, 2).reshape(ROWS, HEADS * HEAD)


def solution(mesh):
    fine = Mesh(mesh.devices.reshape(SIZES), AXES)
    tokens = P(AXES, None)
    return jax.shard_map(
        body,
        mesh=fine,
        in_specs=(tokens, tokens, tokens, P(None, AXES, None), P()),
        out_specs=tokens,
        check_vma=False,
    )
```

time: 82.9 us -> 79.9 us (0.964)
  Pallas kernels: 8.57 us -> 5.21 us
  waiting for transfers between devices: 2.26 us -> 0.01 us
  other arithmetic: 0.03 us -> 1.9 us
    pallas_call x3 -> x2, Pallas kernels: 8.57 us -> 5.21 us  [attend(): pl.pallas_call(functools.partial(attend_kernel, its_core, bool(state)), o...]
    ppermute x1, waiting for transfers between devices: 2.26 us -> 0.01 us  [body(): far = lax.ppermute(near, 'core', [(0, 1), (1, 0)])]
    reshape x0 -> x1, other arithmetic: none -> 1.16 us  [pack(): packed = scaled.transpose(2, 0, 1, 3).reshape(HEADS, 3 * ROWS, HEAD)]
  transfers between devices with their start and end apart: 1 -> 1, of which waited for: 1 -> 0; matrix products, arithmetic and copies ran while one was open for 0% -> 0% of each run, Pallas kernels for 0% -> 3%
where the time goes in v2:
time: 79.9 us; the launch traced here: 79.6 us
  blocking collectives  64.6 us (81%)
  starting transfers between devices  6.78 us (8%)
  Pallas kernels  5.21 us (7%)
  other arithmetic  1.9 us (2%)
  local copies, waits for them, and re-layouts  1.01 us (1%)
    all_to_all x1, blocking collectives, body(): mine = lax.all_to_all(packed, ('z', 'y'), 0, 0, tiled=True)  32 us
    all_to_all x1, blocking collectives, body(): lax.all_to_all(attended.reshape(SLOTS, ROWS, HEAD), ('z', 'y'), 0, 0, til...  17.5 us
    all_to_all x1, blocking collectives, body(): lax.all_to_all(jnp.broadcast_to(own, (4, 2, OWN, HEAD)), X, 0, 0, tiled=T...  15.1 us
    ppermute x1, starting transfers between devices, body(): far = lax.ppermute(near, 'core', [(0, 1), (1, 0)])  6.78 us
    pallas_call x2, Pallas kernels, attend(): pl.pallas_call(functools.partial(attend_kernel, its_core, bool(state)), o...  5.21 us
  transfers between devices with their start and end apart: 1, of which 0 were waited for; matrix products, arithmetic and copies ran while one was open for 0% of the time, Pallas kernels for 3%

profile of v2, /device:TPU:1, one launch (start us, length us, event | category | flops | bytes accessed | tf_op | source)
XLA Modules:
  0.0 79.6 jit_solution(5057020310148461383)
XLA Ops:
  0.0 0.0 copy-start.1
  0.0 0.7 multiply_exponential_fusion
  0.8 0.1 copy.6
  0.8 0.1 copy-done.1
  0.9 1.2 %copy_bitcast_fusion = bf16[48,24,128]{2,1,0:T(8,128)(2,1)S(1)} fusion(bf16[1,8,48,128]{3,1,2,0:T(8,128)(2,1)S(1)} %bitcast.23, bf16[1,8,48,128]{3,1,2,0:T(8,128)(2,1)} %bitcast.24, bf16[1,8,48,128]{3,1,2,0:T(8,128)(2,1)} %bitcast.25, f32[3,8,48]{1,2,0:T(8,128)S(1)} %copy.6), kind=kLoop, calls=%fused_computation.2 | loop fusion | flops 737280 | bytes 594432 | tf_op jit(solution)/shard_map/reshape | solution.py:128
  2.1 32.0 %all_to_all.15 = bf16[64,24,128]{2,1,0:T(8,128)(2,1)S(1)} all-to-all(bf16[64,24,128]{2,1,0:T(8,128)(2,1)S(1)} %pad.4), channel_id=1, replica_groups=mesh['z'=8,'xh'=2,'core'=2,'y'=8,'xl'=2] {'z','y'}, dimensions={0} | all-to-all | bytes 786432 | tf_op jit(solution)/shard_map/all_to_all | solution.py:134
  34.1 0.1 broadcast_in_dim.9
  34.2 15.1 %all_to_all.16.kv_ref = bf16[4,2,512,128]{3,2,1,0:T(8,128)(2,1)S(1)} all-to-all(bf16[4,2,512,128]{3,2,1,0:T(8,128)(2,1)S(1)} %broadcast_in_dim.9), channel_id=1, replica_groups=mesh['z'=8,'xh'=2,'core'=2,'y'=8,'xl'=2] {'xh','xl'}, dimensions={0} | all-to-all | bytes 2097152 | tf_op jit(solution)/shard_map/all_to_all | solution.py:138
  49.4 0.0 copy-start
  49.4 6.8 %collective-permute-start = (bf16[4,2,512,128]{3,2,1,0:T(8,128)(2,1)S(1)}, bf16[4,2,512,128]{3,2,1,0:T(8,128)(2,1)S(1)}, u32[]{:S(2)}, u32[]{:S(2)}) collective-permute-start(bf16[4,2,512,128]{3,2,1,0:T(8,128)(2,1)S(1)} %all_to_all.16.kv_ref), channel_id=1, source_target_pairs={{0,16},{16,0},{1,17},{17,1},{2,18},{18,2},{3,19},{19,3},{4,20},{20... | collective-permute-start | bytes 3145736 | tf_op jit(solution)/shard_map/ppermute | solution.py:139
  56.2 0.0 copy-done
  56.2 2.5 %shard_map.55 = (f32[512,128]{1,0:T(8,128)S(1)}, f32[512,128]{1,0:T(8,128)S(1)}, f32[512,128]{1,0:T(8,128)S(1)}) custom-call(s32[4]{0:T(128)S(1)} %copy-done, bf16[512,128]{1,0:T(8,128)(2,1)S(1)} %slice_bitcast_fusion.1.q_ref, bf16[4,2,512,128]{3,2,1,0:T(8,128)(2,1)S(1)} %all_to_all.16.kv_ref), custom_call_target="tpu_custom_call" | custom-call | flops 536870912 | bytes 1048576 | tf_op jit(solution)/shard_map/pallas_call | solution.py:111
  58.7 0.0 collective-permute-done.kv_ref
  58.7 2.7 %shard_map.56 = bf16[512,128]{1,0:T(8,128)(2,1)S(1)} custom-call(s32[4]{0:T(128)S(1)} %copy-done, bf16[512,128]{1,0:T(8,128)(2,1)S(1)} %slice_bitcast_fusion.1.q_ref, bf16[4,2,512,128]{3,2,1,0:T(8,128)(2,1)S(1)} %collective-permute-done.kv_ref, f32[512,128]{1,0:T(8,128)S(1)} %get-tuple-element.8.refs_0_, f32[512,128]{1,0:T(8,128)S(1)} %get-tuple-element.9.refs_1_, ...), custom_call_target="tpu_custom_call" | custom-call | flops 536870912 | bytes 1048576 | tf_op jit(solution)/shard_map/pallas_call | solution.py:111
  61.4 17.5 %all_to_all.17 = bf16[64,8,128]{2,1,0:T(8,128)(2,1)S(1)} all-to-all(bf16[64,8,128]{2,1,0:T(8,128)(2,1)S(1)} %bitcast.22), channel_id=1, replica_groups=mesh['z'=8,'xh'=2,'core'=2,'y'=8,'xl'=2] {'z','y'}, dimensions={0} | all-to-all | bytes 262144 | tf_op jit(solution)/shard_map/all_to_all | solution.py:142
  78.9 0.6 slice_bitcast_fusion.2
  (3 shorter events, 0.1 us)
Async XLA Ops:
  0.0 0.9 %copy-start.1 = (bf16[8,6144]{1,0:T(8,128)(2,1)S(1)}, bf16[8,6144]{1,0:T(8,128)(2,1)}, u32[]{:S(2)}) copy-start(bf16[8,6144]{1,0:T(8,128)(2,1)} %param.7) | copy-start | bytes 294916
  49.4 6.8 %copy-start = (s32[4]{0:T(128)S(1)}, s32[4]{0:T(128)}, u32[]{:S(2)}) copy-start(s32[4]{0:T(128)} %length_ref.3) | copy-start | bytes 52
  49.4 9.3 %collective-permute-start = (bf16[4,2,512,128]{3,2,1,0:T(8,128)(2,1)S(1)}, bf16[4,2,512,128]{3,2,1,0:T(8,128)(2,1)S(1)}, u32[]{:S(2)}, u32[]{:S(2)}) collective-permute-start(bf16[4,2,512,128]{3,2,1,0:T(8,128)(2,1)S(1)} %all_to_all.16.kv_ref), channel_id=1, source_target_pairs={{0,16},{16,0},{1,17},{17,1},{2,18},{18,2},{3,19},{19,3},{4,20},{20... | collective-permute-start | bytes 3145736 | tf_op jit(solution)/shard_map/ppermute | solution.py:139

commit v3 on v2

v3 whole, which is shorter than its diff:
```python
import functools
import math

import jax
import jax.numpy as jnp
from jax import lax
from jax.experimental import pallas as pl
from jax.experimental.pallas import tpu as pltpu
from jax.sharding import Mesh
from jax.sharding import PartitionSpec as P

AXES = ("z", "xh", "core", "y", "xl")
SIZES = (8, 2, 2, 8, 2)
SLOTS = 64
HEADS = 48
HEAD = 128
ROWS = 8
OWN = SLOTS * ROWS
X = ("xh", "xl")


def clip_of(length_ref, token):
    end = jnp.int32(0)
    clip = jnp.zeros_like(token)
    for i in range(4):
        end = end + length_ref[i]
        clip = clip + (end <= token).astype(jnp.int32)
    return clip


def token_of(row, xh, core, xl):
    z = row // 64
    y = (row // 8) % 8
    return z * 512 + xh * 256 + core * 128 + y * 16 + xl * 8 + row % 8


QB = 256


def attend_kernel(sources, carried, final, length_ref, q_ref, *refs):
    count = len({place for place, _, _, _ in sources})
    kv_refs, refs = refs[:count], refs[count:]
    state_refs, refs = (refs[:3], refs[3:]) if carried else ((), refs)
    out_refs, s_ref = refs[:-1], refs[-1]
    xh, xl, core = lax.axis_index("xh"), lax.axis_index("xl"), lax.axis_index("core")
    factor = math.log2(math.e) / math.sqrt(HEAD)
    key_row = lax.broadcasted_iota(jnp.int32, (1, OWN), 1)
    keys, values, key_clip = [], [], []
    for place, index, hops, cores in sources:
        x = (xh * 2 + xl + 4 - hops) % 4
        its_core = core if cores == 0 else 1 - core
        key_clip.append(clip_of(length_ref, token_of(key_row, x // 2, its_core, x % 2)))
        keys.append(kv_refs[place].at[index, 0])
        values.append(kv_refs[place].at[index, 1])
    blocks, parts = OWN // QB, len(sources)

    def rows(block):
        return slice(block * QB, (block + 1) * QB)

    def begin(block):
        query_row = block * QB + lax.broadcasted_iota(jnp.int32, (QB, 1), 0)
        query_clip = clip_of(length_ref, token_of(query_row, xh, core, xl))
        if carried:
            top = state_refs[1][rows(block), :]
        else:
            top = jnp.full((QB, HEAD), -1e30, jnp.float32)
        return q_ref[rows(block), :], query_clip, top

    def score(block, part, query, query_clip, top):
        scores = lax.dot_general(
            query, keys[part][...], (((1,), (1,)), ((), ())), preferred_element_type=jnp.float32
        )
        scores = jnp.where(query_clip == key_clip[part], scores, -1e30)
        s_ref[block % 2, :, part * OWN : (part + 1) * OWN] = scores
        for j in range(0, OWN, HEAD):
            top = jnp.maximum(top, scores[:, j : j + HEAD])
        return top

    query, query_clip, top = begin(0)
    for part in range(parts):
        top = score(0, part, query, query_clip, top)
    for block in range(blocks):
        highest = jnp.max(top, axis=1, keepdims=True)
        shift = highest * factor
        if carried:
            old = jnp.exp2(state_refs[1][rows(block), :] * factor - shift)
            numerator = state_refs[0][rows(block), :] * old
            total = state_refs[2][rows(block), :] * old
        else:
            total = numerator = jnp.zeros((QB, HEAD), jnp.float32)
        if block + 1 < blocks:
            query, query_clip, top = begin(block + 1)
        for part in range(parts):
            if block + 1 < blocks:
                top = score(block + 1, part, query, query_clip, top)
            scores = s_ref[block % 2, :, part * OWN : (part + 1) * OWN]
            weights = jnp.exp2(scores * factor - shift)
            for j in range(0, OWN, HEAD):
                total = total + weights[:, j : j + HEAD]
            numerator = numerator + jnp.dot(
                weights.astype(jnp.bfloat16), values[part][...], preferred_element_type=jnp.float32
            )
        if final:
            out_refs[0][rows(block), :] = (
                numerator / jnp.sum(total, axis=1, keepdims=True)
            ).astype(jnp.bfloat16)
        else:
            out_refs[0][rows(block), :] = numerator
            out_refs[1][rows(block), :] = jnp.broadcast_to(highest, (QB, HEAD))
            out_refs[2][rows(block), :] = total


VMEM = pl.BlockSpec(memory_space=pltpu.VMEM)
SMEM = pl.BlockSpec(memory_space=pltpu.SMEM)


def attend(sources, final, lengths, query, kvs, state=()):
    f32 = jax.ShapeDtypeStruct((OWN, HEAD), jnp.float32)
    keys = len(sources) * OWN
    return pl.pallas_call(
        functools.partial(attend_kernel, sources, bool(state), final),
        out_shape=jax.ShapeDtypeStruct((OWN, HEAD), jnp.bfloat16) if final else [f32] * 3,
        in_specs=[SMEM] + [VMEM] * (1 + len(kvs) + len(state)),
        out_specs=VMEM if final else [VMEM] * 3,
        scratch_shapes=[pltpu.VMEM((2, QB, keys), jnp.float32)],
        compiler_params=pltpu.CompilerParams(vmem_limit_bytes=32 * 2**20),
        cost_estimate=pl.CostEstimate(
            flops=4 * OWN * keys * HEAD, bytes_accessed=2**20, transcendentals=OWN * keys
        ),
    )(lengths, query, *kvs, *state)


def pack(q_payload, k_payload, v_payload, exponents):
    scale = jnp.exp2(exponents.astype(jnp.float32))
    payload = jnp.stack([q_payload, k_payload, v_payload]).reshape(3, ROWS, HEADS, HEAD)
    scaled = (payload.astype(jnp.float32) * scale[:, :, :, None]).astype(jnp.bfloat16)
    packed = scaled.transpose(2, 0, 1, 3).reshape(HEADS, 3 * ROWS, HEAD)
    return jnp.pad(packed, ((0, SLOTS - HEADS), (0, 0), (0, 0)))


def body(q_payload, k_payload, v_payload, exponents, lengths):
    packed = pack(q_payload, k_payload, v_payload, exponents)
    mine = lax.all_to_all(packed, ("z", "y"), 0, 0, tiled=True)
    query = mine[:, :ROWS].reshape(OWN, HEAD)
    own = mine[:, ROWS:].reshape(1, SLOTS, 2, ROWS, HEAD).transpose(0, 2, 1, 3, 4)
    own = own.reshape(1, 2, OWN, HEAD)
    swap = [(0, 1), (1, 0)]
    hops = (1, 3, 2)
    near = [lax.ppermute(own, X, [(x, (x + hop) % 4) for x in range(4)]) for hop in hops]
    sibling = lax.ppermute(own, "core", swap)
    state = attend(((0, 0, 0, 0), (1, 0, 0, 1)), False, lengths, query, (own, sibling))
    near, state = lax.optimization_barrier((near, state))
    far = lax.ppermute(jnp.concatenate(near), "core", swap)
    places = tuple((i, 0, hop, 0) for i, hop in enumerate(hops))
    state = attend(places, False, lengths, query, near, state)
    places = tuple((0, i, hop, 1) for i, hop in enumerate(hops))
    attended = attend(places, True, lengths, query, (far,), state)
    back = lax.all_to_all(attended.reshape(SLOTS, ROWS, HEAD), ("z", "y"), 0, 0, tiled=True)
    return back[:HEADS].transpose(1, 0, 2).reshape(ROWS, HEADS * HEAD)


def solution(mesh):
    fine = Mesh(mesh.devices.reshape(SIZES), AXES)
    tokens = P(AXES, None)
    return jax.shard_map(
        body,
        mesh=fine,
        in_specs=(tokens, tokens, tokens, P(None, AXES, None), P()),
        out_specs=tokens,
        check_vma=False,
    )
```

time: 79.9 us -> 81.9 us (1.025)
  blocking collectives: 64.6 us -> 47.7 us
  starting transfers between devices: 6.78 us -> 18.4 us
  waiting for transfers between devices: 0.01 us -> 6.1 us
  Pallas kernels: 5.21 us -> 6.28 us
    all_to_all x1 -> x0, blocking collectives: 15.1 us -> none  [body(): lax.all_to_all(jnp.broadcast_to(own, (4, 2, OWN, HEAD)), X, 0, 0, tiled=T...]
    ppermute x1 -> x5, starting transfers between devices: 6.78 us -> 18.4 us  [the longest x3 9.93 us: body(): lax.ppermute(own, X, [(x, (x + hop) % 4) for x in range(4)])]
    ppermute x1 -> x5, waiting for transfers between devices: 0.01 us -> 6.1 us  [the longest x3 6.09 us: body(): lax.ppermute(own, X, [(x, (x + hop) % 4) for x in range(4)])]
    all_to_all x1, blocking collectives: 17.5 us -> 15.8 us  [body(): lax.all_to_all(attended.reshape(SLOTS, ROWS, HEAD), ('z', 'y'), 0, 0, til...]
    pallas_call x2 -> x3, Pallas kernels: 5.21 us -> 6.28 us  [attend(): pl.pallas_call(functools.partial(attend_kernel, sources, bool(state), fin...]
  transfers between devices with their start and end apart: 1 -> 5, of which waited for: 0 -> 2; matrix products, arithmetic and copies ran while one was open for 0% -> 0% of each run, Pallas kernels for 3% -> 5%
where the time goes in v3:
time: 81.9 us; the launch traced here: 81.6 us
  blocking collectives  47.7 us (58%)
  starting transfers between devices  18.4 us (22%)
  Pallas kernels  6.28 us (8%)
  waiting for transfers between devices  6.1 us (7%)
  other arithmetic  1.99 us (2%)
  local copies, waits for them, and re-layouts  0.87 us (1%)
    all_to_all x1, blocking collectives, body(): mine = lax.all_to_all(packed, ('z', 'y'), 0, 0, tiled=True)  32 us
    all_to_all x1, blocking collectives, body(): lax.all_to_all(attended.reshape(SLOTS, ROWS, HEAD), ('z', 'y'), 0, 0, til...  15.8 us
    ppermute x3, starting transfers between devices, body(): lax.ppermute(own, X, [(x, (x + hop) % 4) for x in range(4)])  9.93 us
    pallas_call x3, Pallas kernels, attend(): pl.pallas_call(functools.partial(attend_kernel, sources, bool(state), fin...  6.28 us
    ppermute x3, waiting for transfers between devices, body(): lax.ppermute(own, X, [(x, (x + hop) % 4) for x in range(4)])  6.09 us
    ppermute x1, starting transfers between devices, body(): sibling = lax.ppermute(own, 'core', swap)  5.17 us
    ppermute x1, starting transfers between devices, body(): far = lax.ppermute(jnp.concatenate(near), 'core', swap)  3.34 us
  transfers between devices with their start and end apart: 5, of which 2 were waited for; matrix products, arithmetic and copies ran while one was open for 0% of the time, Pallas kernels for 5%

profile of v3, /device:TPU:1, one launch (start us, length us, event | category | flops | bytes accessed | tf_op | source)
XLA Modules:
  0.0 81.6 jit_solution(13831795176823876895)
XLA Ops:
  0.0 0.0 copy-start.1
  0.0 0.7 multiply_exponential_fusion
  0.8 0.1 copy.11
  0.9 0.1 copy-done.1
  0.9 1.2 %fusion = bf16[48,24,128]{2,1,0:T(8,128)(2,1)S(1)} fusion(bf16[1,8,48,128]{3,1,0,2:T(8,128)(2,1)S(1)} %bitcast.28, bf16[1,8,48,128]{3,1,0,2:T(8,128)(2,1)} %bitcast.29, bf16[1,8,48,128]{3,1,0,2:T(8,128)(2,1)} %bitcast.30, f32[3,8,48]{1,0,2:T(4,128)S(1)} %copy.11), kind=kLoop, calls=%fused_computation.2 | loop fusion | flops 737280 | bytes 594432 | tf_op jit(solution)/shard_map/reshape | solution.py:137
  2.1 32.0 %all_to_all.10 = bf16[64,24,128]{2,1,0:T(8,128)(2,1)S(1)} all-to-all(bf16[64,24,128]{2,1,0:T(8,128)(2,1)S(1)} %pad.4), channel_id=1, replica_groups=mesh['z'=8,'xh'=2,'core'=2,'y'=8,'xl'=2] {'z','y'}, dimensions={0} | all-to-all | bytes 786432 | tf_op jit(solution)/shard_map/all_to_all | solution.py:143
  34.1 0.0 copy-start
  34.1 5.2 %collective-permute-start.3 = (bf16[1,2,512,128]{3,2,1,0:T(8,128)(2,1)S(1)}, bf16[1,2,512,128]{3,2,1,0:T(8,128)(2,1)S(1)}, u32[]{:S(2)}, u32[]{:S(2)}) collective-permute-start(bf16[1,2,512,128]{3,2,1,0:T(8,128)(2,1)S(1)} %copy_bitcast_fusion.refs_0_), channel_id=1, source_target_pairs={{0,16},{16,0},{1,17},{17,1},{2,18},{18,2},{3,19},{19,3},{4,20},{20... | collective-permute-start | bytes 786440 | tf_op jit(solution)/shard_map/ppermute | solution.py:150
  39.3 4.7 %collective-permute-start.2 = (bf16[1,2,512,128]{3,2,1,0:T(8,128)(2,1)S(1)}, bf16[1,2,512,128]{3,2,1,0:T(8,128)(2,1)S(1)}, u32[]{:S(2)}, u32[]{:S(2)}) collective-permute-start(bf16[1,2,512,128]{3,2,1,0:T(8,128)(2,1)S(1)} %copy_bitcast_fusion.refs_0_), channel_id=1, source_target_pairs={{0,32},{1,33},{32,0},{33,1},{2,34},{3,35},{34,2},{35,3},{4,36},{5,... | collective-permute-start | bytes 786440 | tf_op jit(solution)/shard_map/ppermute | solution.py:149
  43.9 2.8 %collective-permute-start.1 = (bf16[1,2,512,128]{3,2,1,0:T(8,128)(2,1)S(1)}, bf16[1,2,512,128]{3,2,1,0:T(8,128)(2,1)S(1)}, u32[]{:S(2)}, u32[]{:S(2)}) collective-permute-start(bf16[1,2,512,128]{3,2,1,0:T(8,128)(2,1)S(1)} %copy_bitcast_fusion.refs_0_), channel_id=1, source_target_pairs={{0,33},{1,0},{32,1},{33,32},{2,35},{3,2},{34,3},{35,34},{4,37},{5,... | collective-permute-start | bytes 786440 | tf_op jit(solution)/shard_map/ppermute | solution.py:149
  46.7 2.5 %collective-permute-start = (bf16[1,2,512,128]{3,2,1,0:T(8,128)(2,1)S(1)}, bf16[1,2,512,128]{3,2,1,0:T(8,128)(2,1)S(1)}, u32[]{:S(2)}, u32[]{:S(2)}) collective-permute-start(bf16[1,2,512,128]{3,2,1,0:T(8,128)(2,1)S(1)} %copy_bitcast_fusion.refs_0_), channel_id=1, source_target_pairs={{0,1},{1,32},{32,33},{33,0},{2,3},{3,34},{34,35},{35,2},{4,5},{5,3... | collective-permute-start | bytes 786440 | tf_op jit(solution)/shard_map/ppermute | solution.py:149
  49.3 0.0 collective-permute-done.3.refs_1_
  49.3 0.0 copy-done
  49.3 1.7 %shard_map.55 = (f32[512,128]{1,0:T(8,128)S(1)}, f32[512,128]{1,0:T(8,128)S(1)}, f32[512,128]{1,0:T(8,128)S(1)}) custom-call(s32[4]{0:T(128)S(1)} %copy-done, bf16[512,128]{1,0:T(8,128)(2,1)S(1)} %slice_bitcast_fusion.1.q_ref, bf16[1,2,512,128]{3,2,1,0:T(8,128)(2,1)S(1)} %copy_bitcast_fusion.refs_0_, bf16[1,2,512,128]{3,2,1,0:T(8,128)(2,1)S(1)} %collective-permute-done.3.refs_1_), custom_call_target="tpu_custom_call" | custom-call | flops 268435456 | bytes 1048576 | tf_op jit(solution)/shard_map/pallas_call | solution.py:120
  51.0 0.0 collective-permute-done.2.refs_2_
  51.0 5.3 %collective-permute-done.1.refs_1_ = bf16[1,2,512,128]{3,2,1,0:T(8,128)(2,1)S(1)} collective-permute-done((bf16[1,2,512,128]{3,2,1,0:T(8,128)(2,1)S(1)}, bf16[1,2,512,128]{3,2,1,0:T(8,128)(2,1)S(1)}, u32[]{:S(2)}, u32[]{:S(2)}) %collective-permute-start.1) | collective-permute-done | bytes 262176 | tf_op jit(solution)/shard_map/ppermute | solution.py:149
  56.4 0.8 collective-permute-done.refs_0_
  57.1 0.1 pad_maximum_fusion
  57.2 3.3 %collective-permute-start.4 = (bf16[3,2,512,128]{3,2,1,0:T(8,128)(2,1)S(1)}, bf16[3,2,512,128]{3,2,1,0:T(8,128)(2,1)S(1)}, u32[]{:S(2)}, u32[]{:S(2)}) collective-permute-start(bf16[3,2,512,128]{3,2,1,0:T(8,128)(2,1)S(1)} %pad_maximum_fusion), channel_id=1, source_target_pairs={{0,16},{16,0},{1,17},{17,1},{2,18},{18,2},{3,19},{19,3},{4,20},{20... | collective-permute-start | bytes 2359304 | tf_op jit(solution)/shard_map/ppermute | solution.py:153
  60.6 2.2 %shard_map.56 = (f32[512,128]{1,0:T(8,128)S(1)}, f32[512,128]{1,0:T(8,128)S(1)}, f32[512,128]{1,0:T(8,128)S(1)}) custom-call(s32[4]{0:T(128)S(1)} %copy-done, bf16[512,128]{1,0:T(8,128)(2,1)S(1)} %slice_bitcast_fusion.1.q_ref, bf16[1,2,512,128]{3,2,1,0:T(8,128)(2,1)S(1)} %collective-permute-done.refs_0_, ...), custom_call_target="tpu_custom_call" | custom-call | flops 402653184 | bytes 1048576 | tf_op jit(solution)/shard_map/pallas_call | solution.py:120
  62.8 0.0 collective-permute-done.4.refs_0_
  62.8 2.3 %shard_map.57 = bf16[512,128]{1,0:T(8,128)(2,1)S(1)} custom-call(s32[4]{0:T(128)S(1)} %copy-done, bf16[512,128]{1,0:T(8,128)(2,1)S(1)} %slice_bitcast_fusion.1.q_ref, bf16[3,2,512,128]{3,2,1,0:T(8,128)(2,1)S(1)} %collective-permute-done.4.refs_0_, f32[512,128]{1,0:T(8,128)S(1)} %get-tuple-element.26.refs_1_, f32[512,128]{1,0:T(8,128)S(1)} %get-tuple-element.27.refs_2_, ...), custom_call_target="tpu_custom_call" | custom-call | flops 402653184 | bytes 1048576 | tf_op jit(solution)/shard_map/pallas_call | solution.py:120
  65.1 15.8 %all_to_all.11 = bf16[64,8,128]{2,1,0:T(8,128)(2,1)S(1)} all-to-all(bf16[64,8,128]{2,1,0:T(8,128)(2,1)S(1)} %bitcast.27), channel_id=1, replica_groups=mesh['z'=8,'xh'=2,'core'=2,'y'=8,'xl'=2] {'z','y'}, dimensions={0} | all-to-all | bytes 262144 | tf_op jit(solution)/shard_map/all_to_all | solution.py:158
  80.9 0.6 slice_bitcast_fusion.2
  (3 shorter events, 0.1 us)
Async XLA Ops:
  0.0 0.9 %copy-start.1 = (bf16[8,6144]{1,0:T(8,128)(2,1)S(1)}, bf16[8,6144]{1,0:T(8,128)(2,1)}, u32[]{:S(2)}) copy-start(bf16[8,6144]{1,0:T(8,128)(2,1)} %param.7) | copy-start | bytes 294916
  34.1 15.2 %copy-start = (s32[4]{0:T(128)S(1)}, s32[4]{0:T(128)}, u32[]{:S(2)}) copy-start(s32[4]{0:T(128)} %length_ref.5) | copy-start | bytes 52
  34.1 15.2 %collective-permute-start.3 = (bf16[1,2,512,128]{3,2,1,0:T(8,128)(2,1)S(1)}, bf16[1,2,512,128]{3,2,1,0:T(8,128)(2,1)S(1)}, u32[]{:S(2)}, u32[]{:S(2)}) collective-permute-start(bf16[1,2,512,128]{3,2,1,0:T(8,128)(2,1)S(1)} %copy_bitcast_fusion.refs_0_), channel_id=1, source_target_pairs={{0,16},{16,0},{1,17},{17,1},{2,18},{18,2},{3,19},{19,3},{4,20},{20... | collective-permute-start | bytes 786440 | tf_op jit(solution)/shard_map/ppermute | solution.py:150
  39.3 11.7 %collective-permute-start.2 = (bf16[1,2,512,128]{3,2,1,0:T(8,128)(2,1)S(1)}, bf16[1,2,512,128]{3,2,1,0:T(8,128)(2,1)S(1)}, u32[]{:S(2)}, u32[]{:S(2)}) collective-permute-start(bf16[1,2,512,128]{3,2,1,0:T(8,128)(2,1)S(1)} %copy_bitcast_fusion.refs_0_), channel_id=1, source_target_pairs={{0,32},{1,33},{32,0},{33,1},{2,34},{3,35},{34,2},{35,3},{4,36},{5,... | collective-permute-start | bytes 786440 | tf_op jit(solution)/shard_map/ppermute | solution.py:149
  43.9 12.4 %collective-permute-start.1 = (bf16[1,2,512,128]{3,2,1,0:T(8,128)(2,1)S(1)}, bf16[1,2,512,128]{3,2,1,0:T(8,128)(2,1)S(1)}, u32[]{:S(2)}, u32[]{:S(2)}) collective-permute-start(bf16[1,2,512,128]{3,2,1,0:T(8,128)(2,1)S(1)} %copy_bitcast_fusion.refs_0_), channel_id=1, source_target_pairs={{0,33},{1,0},{32,1},{33,32},{2,35},{3,2},{34,3},{35,34},{4,37},{5,... | collective-permute-start | bytes 786440 | tf_op jit(solution)/shard_map/ppermute | solution.py:149
  46.7 10.4 %collective-permute-start = (bf16[1,2,512,128]{3,2,1,0:T(8,128)(2,1)S(1)}, bf16[1,2,512,128]{3,2,1,0:T(8,128)(2,1)S(1)}, u32[]{:S(2)}, u32[]{:S(2)}) collective-permute-start(bf16[1,2,512,128]{3,2,1,0:T(8,128)(2,1)S(1)} %copy_bitcast_fusion.refs_0_), channel_id=1, source_target_pairs={{0,1},{1,32},{32,33},{33,0},{2,3},{3,34},{34,35},{35,2},{4,5},{5,3... | collective-permute-start | bytes 786440 | tf_op jit(solution)/shard_map/ppermute | solution.py:149
  57.2 5.6 %collective-permute-start.4 = (bf16[3,2,512,128]{3,2,1,0:T(8,128)(2,1)S(1)}, bf16[3,2,512,128]{3,2,1,0:T(8,128)(2,1)S(1)}, u32[]{:S(2)}, u32[]{:S(2)}) collective-permute-start(bf16[3,2,512,128]{3,2,1,0:T(8,128)(2,1)S(1)} %pad_maximum_fusion), channel_id=1, source_target_pairs={{0,16},{16,0},{1,17},{17,1},{2,18},{18,2},{3,19},{19,3},{4,20},{20... | collective-permute-start | bytes 2359304 | tf_op jit(solution)/shard_map/ppermute | solution.py:153

commit v4 on v2

--- a/solution.py
+++ b/solution.py
@@ -3,20 +3,30 @@
 
 import jax
 import jax.numpy as jnp
+import numpy as np
 from jax import lax
 from jax.experimental import pallas as pl
 from jax.experimental.pallas import tpu as pltpu
 from jax.sharding import Mesh
 from jax.sharding import PartitionSpec as P
 
-AXES = ("z", "xh", "core", "y", "xl")
 SIZES = (8, 2, 2, 8, 2)
 SLOTS = 64
 HEADS = 48
 HEAD = 128
 ROWS = 8
 OWN = SLOTS * ROWS
-X = ("xh", "xl")
+FIRST_Z, FIRST_Y = 5, 4
+X_ORDER = [2, 3, 0, 1]
+PLACES = np.arange(512).reshape(SIZES)
+BY_HEAD = np.roll(PLACES, (-FIRST_Z, -FIRST_Y), (0, 3)).transpose(1, 2, 4, 0, 3).reshape(8, SLOTS)
+BY_X = PLACES.transpose(0, 2, 3, 1, 4).reshape(128, 4)[:, X_ORDER]
+BY_CORE = PLACES.transpose(0, 1, 3, 4, 2).reshape(256, 2)
+
+
+def place():
+    index = lax.axis_index("device")
+    return (index // 32) % 2, index % 2, (index // 16) % 2
 
 
 def clip_of(length_ref, token):
@@ -29,8 +39,8 @@
 
 
 def token_of(row, xh, core, xl):
-    z = row // 64
-    y = (row // 8) % 8
+    z = (row // 64 + FIRST_Z) % 8
+    y = (row // 8 + FIRST_Y) % 8
     return z * 512 + xh * 256 + core * 128 + y * 16 + xl * 8 + row % 8
 
 
@@ -42,12 +52,12 @@
         acc_ref, top_ref, sum_ref, out_ref, s_ref = refs
     else:
         acc_ref, top_ref, sum_ref, s_ref = refs
-    xh, xl, core = lax.axis_index("xh"), lax.axis_index("xl"), lax.axis_index("core")
+    xh, xl, core = place()
     key_core = core if its_core else 1 - core
     factor = math.log2(math.e) / math.sqrt(HEAD)
     key_row = lax.broadcasted_iota(jnp.int32, (1, OWN), 1)
     key_clip = [
-        clip_of(length_ref, token_of(key_row, x // 2, key_core, x % 2)) for x in range(4)
+        clip_of(length_ref, token_of(key_row, x // 2, key_core, x % 2)) for x in X_ORDER
     ]
     blocks = OWN // QB
 
@@ -122,34 +132,39 @@
 
 
 def pack(q_payload, k_payload, v_payload, exponents):
-    scale = jnp.exp2(exponents.astype(jnp.float32))
-    payload = jnp.stack([q_payload, k_payload, v_payload]).reshape(3, ROWS, HEADS, HEAD)
-    scaled = (payload.astype(jnp.float32) * scale[:, :, :, None]).astype(jnp.bfloat16)
-    packed = scaled.transpose(2, 0, 1, 3).reshape(HEADS, 3 * ROWS, HEAD)
-    return jnp.pad(packed, ((0, SLOTS - HEADS), (0, 0), (0, 0)))
+    scale = jnp.exp2(exponents.astype(jnp.float32)).astype(jnp.bfloat16).reshape(3 * ROWS, HEADS)
+    lane_head = jnp.arange(HEADS * HEAD) // HEAD
+    spread = (jnp.arange(HEADS)[:, None] == lane_head[None, :]).astype(jnp.bfloat16)
+    scale = jnp.dot(scale, spread, preferred_element_type=jnp.float32)
+    payload = jnp.concatenate([q_payload, k_payload, v_payload]).astype(jnp.float32)
+    packed = (payload * scale).astype(jnp.bfloat16).reshape(3 * ROWS, HEADS, HEAD)
+    return jnp.pad(packed.transpose(1, 0, 2), ((0, SLOTS - HEADS), (0, 0), (0, 0)))
+
+
+def exchange(array, groups):
+    return lax.all_to_all(array, "device", 0, 0, axis_index_groups=groups.tolist(), tiled=True)
 
 
 def body(q_payload, k_payload, v_payload, exponents, lengths):
     packed = pack(q_payload, k_payload, v_payload, exponents)
-    mine = lax.all_to_all(packed, ("z", "y"), 0, 0, tiled=True)
+    mine = exchange(packed, BY_HEAD)
     query = mine[:, :ROWS].reshape(OWN, HEAD)
     own = mine[:, ROWS:].reshape(1, SLOTS, 2, ROWS, HEAD).transpose(0, 2, 1, 3, 4)
     own = own.reshape(1, 2, OWN, HEAD)
-    near = lax.all_to_all(jnp.broadcast_to(own, (4, 2, OWN, HEAD)), X, 0, 0, tiled=True)
-    far = lax.ppermute(near, "core", [(0, 1), (1, 0)])
+    near = exchange(jnp.broadcast_to(own, (4, 2, OWN, HEAD)), BY_X)
+    far = lax.ppermute(near, "device", [(a, b) for a, b in BY_CORE.tolist()] + [(b, a) for a, b in BY_CORE.tolist()])
     state = attend(True, lengths, query, near)
     attended = attend(False, lengths, query, far, state)
-    back = lax.all_to_all(attended.reshape(SLOTS, ROWS, HEAD), ("z", "y"), 0, 0, tiled=True)
+    back = exchange(attended.reshape(SLOTS, ROWS, HEAD), BY_HEAD)
     return back[:HEADS].transpose(1, 0, 2).reshape(ROWS, HEADS * HEAD)
 
 
 def solution(mesh):
-    fine = Mesh(mesh.devices.reshape(SIZES), AXES)
-    tokens = P(AXES, None)
+    tokens = P("device", None)
     return jax.shard_map(
         body,
-        mesh=fine,
-        in_specs=(tokens, tokens, tokens, P(None, AXES, None), P()),
+        mesh=Mesh(mesh.devices.reshape(-1), ("device",)),
+        in_specs=(tokens, tokens, tokens, P(None, "device", None), P()),
         out_specs=tokens,
         check_vma=False,
     )

time: 79.9 us -> 73 us (0.914)
  blocking collectives: 64.6 us -> 60.2 us
  starting transfers between devices: 6.78 us -> 4.75 us
  other arithmetic: 1.9 us -> 0.01 us
  matrix products: 0 us -> 1.31 us
    all_to_all x3, blocking collectives: 64.6 us -> 60.2 us  [exchange(): lax.all_to_all(array, 'device', 0, 0, axis_index_groups=groups.tolist(),...]
    ppermute x1, starting transfers between devices: 6.78 us -> 4.75 us  [body(): lax.ppermute(near, 'device', [(a, b) for a, b in BY_CORE.tolist()] + [(b,...]
    dot_general x0 -> x1, matrix products: none -> 1.31 us  [pack(): scale = jnp.dot(scale, spread, preferred_element_type=jnp.float32)]
    reshape x1 -> x0, other arithmetic: 1.16 us -> none  [pack(): packed = scaled.transpose(2, 0, 1, 3).reshape(HEADS, 3 * ROWS, HEAD)]
  transfers between devices with their start and end apart: 1 -> 1, of which waited for: 0 -> 0; matrix products, arithmetic and copies ran while one was open for 0% -> 0% of each run, Pallas kernels for 3% -> 4%
where the time goes in v4:
time: 73 us; the launch traced here: 72.8 us
  blocking collectives  60.2 us (82%)
  Pallas kernels  5.53 us (8%)
  starting transfers between devices  4.75 us (7%)
  matrix products  1.31 us (2%)
  local copies, waits for them, and re-layouts  0.91 us (1%)
    all_to_all x3, blocking collectives, exchange(): lax.all_to_all(array, 'device', 0, 0, axis_index_groups=groups.tolist(),...  60.2 us
    pallas_call x2, Pallas kernels, attend(): pl.pallas_call(functools.partial(attend_kernel, its_core, bool(state)), o...  5.53 us
    ppermute x1, starting transfers between devices, body(): lax.ppermute(near, 'device', [(a, b) for a, b in BY_CORE.tolist()] + [(b,...  4.75 us
  transfers between devices with their start and end apart: 1, of which 0 were waited for; matrix products, arithmetic and copies ran while one was open for 0% of the time, Pallas kernels for 4%

profile of v4, /device:TPU:1, one launch (start us, length us, event | category | flops | bytes accessed | tf_op | source)
XLA Modules:
  0.0 72.8 jit_solution(6904026201667249205)
XLA Ops:
  0.0 1.3 %fusion.1 = bf16[3,48,8,128]{3,2,1,0:T(8,128)(2,1)S(1)} fusion(s32[6144]{0:T(1024)S(1)} %add_select_fusion, bf16[8,6144]{1,0:T(8,128)(2,1)} %param.7, bf16[8,6144]{1,0:T(8,128)(2,1)} %param.6, bf16[8,6144]{1,0:T(8,128)(2,1)} %param.5, s32[3,8,48]{2,1,0:T(8,128)} %param.8), kind=kOutput, calls=%fused_computation.3 | convolution fusion | flops 15633792 | bytes 619008 | tf_op jit(solution)/shard_map/dot_general | solution.py:138
  1.3 0.1 copy.11
  1.4 28.3 %all_to_all.15 = bf16[64,24,128]{2,1,0:T(8,128)(2,1)S(1)} all-to-all(bf16[64,24,128]{2,1,0:T(8,128)(2,1)S(1)} %pad.4), channel_id=1, replica_groups={{328,330,332,334,320,322,324,326,392,394,396,398,384,386,388,390,456,45..., dimensions={0} | all-to-all | bytes 786432 | tf_op jit(solution)/shard_map/all_to_all | solution.py:145
  29.7 0.1 broadcast_in_dim.10
  29.9 0.0 copy-start
  29.9 15.7 %all_to_all.16.kv_ref = bf16[4,2,512,128]{3,2,1,0:T(8,128)(2,1)S(1)} all-to-all(bf16[4,2,512,128]{3,2,1,0:T(8,128)(2,1)S(1)} %broadcast_in_dim.10), channel_id=1, replica_groups={{32,33,0,1},{34,35,2,3},{36,37,4,5},{38,39,6,7},{40,41,8,9},{42,43,10,1..., dimensions={0} | all-to-all | bytes 2097152 | tf_op jit(solution)/shard_map/all_to_all | solution.py:145
  45.6 4.7 %collective-permute-start = (bf16[4,2,512,128]{3,2,1,0:T(8,128)(2,1)S(1)}, bf16[4,2,512,128]{3,2,1,0:T(8,128)(2,1)S(1)}, u32[]{:S(2)}, u32[]{:S(2)}) collective-permute-start(bf16[4,2,512,128]{3,2,1,0:T(8,128)(2,1)S(1)} %all_to_all.16.kv_ref), channel_id=1, source_target_pairs={{0,16},{1,17},{2,18},{3,19},{4,20},{5,21},{6,22},{7,23},{8,24},{9,... | collective-permute-start | bytes 3145736 | tf_op jit(solution)/shard_map/ppermute | solution.py:155
  50.3 0.0 copy-done
  50.4 2.7 %shard_map.55 = (f32[512,128]{1,0:T(8,128)S(1)}, f32[512,128]{1,0:T(8,128)S(1)}, f32[512,128]{1,0:T(8,128)S(1)}) custom-call(s32[4]{0:T(128)S(1)} %copy-done, bf16[512,128]{1,0:T(8,128)(2,1)S(1)} %slice_bitcast_fusion.1.q_ref, bf16[4,2,512,128]{3,2,1,0:T(8,128)(2,1)S(1)} %all_to_all.16.kv_ref), custom_call_target="tpu_custom_call" | custom-call | flops 536870912 | bytes 1048576 | tf_op jit(solution)/shard_map/pallas_call | solution.py:121
  53.0 0.0 collective-permute-done.kv_ref
  53.1 2.9 %shard_map.56 = bf16[512,128]{1,0:T(8,128)(2,1)S(1)} custom-call(s32[4]{0:T(128)S(1)} %copy-done, bf16[512,128]{1,0:T(8,128)(2,1)S(1)} %slice_bitcast_fusion.1.q_ref, bf16[4,2,512,128]{3,2,1,0:T(8,128)(2,1)S(1)} %collective-permute-done.kv_ref, f32[512,128]{1,0:T(8,128)S(1)} %get-tuple-element.8.refs_0_, f32[512,128]{1,0:T(8,128)S(1)} %get-tuple-element.9.refs_1_, ...), custom_call_target="tpu_custom_call" | custom-call | flops 536870912 | bytes 1048576 | tf_op jit(solution)/shard_map/pallas_call | solution.py:121
  55.9 16.2 %all_to_all.17 = bf16[64,8,128]{2,1,0:T(8,128)(2,1)S(1)} all-to-all(bf16[64,8,128]{2,1,0:T(8,128)(2,1)S(1)} %bitcast.25), channel_id=1, replica_groups={{328,330,332,334,320,322,324,326,392,394,396,398,384,386,388,390,456,45..., dimensions={0} | all-to-all | bytes 262144 | tf_op jit(solution)/shard_map/all_to_all | solution.py:145
  72.1 0.6 slice_bitcast_fusion.2
  (4 shorter events, 0.1 us)
Async XLA Ops:
  29.9 20.5 %copy-start = (s32[4]{0:T(128)S(1)}, s32[4]{0:T(128)}, u32[]{:S(2)}) copy-start(s32[4]{0:T(128)} %length_ref.3) | copy-start | bytes 52
  45.6 7.5 %collective-permute-start = (bf16[4,2,512,128]{3,2,1,0:T(8,128)(2,1)S(1)}, bf16[4,2,512,128]{3,2,1,0:T(8,128)(2,1)S(1)}, u32[]{:S(2)}, u32[]{:S(2)}) collective-permute-start(bf16[4,2,512,128]{3,2,1,0:T(8,128)(2,1)S(1)} %all_to_all.16.kv_ref), channel_id=1, source_target_pairs={{0,16},{1,17},{2,18},{3,19},{4,20},{5,21},{6,22},{7,23},{8,24},{9,... | collective-permute-start | bytes 3145736 | tf_op jit(solution)/shard_map/ppermute | solution.py:155

commit v5 on v4

--- a/solution.py
+++ b/solution.py
@@ -17,9 +17,9 @@
 ROWS = 8
 OWN = SLOTS * ROWS
 FIRST_Z, FIRST_Y = 5, 4
-X_ORDER = [2, 3, 0, 1]
+X_ORDER = [2, 0, 3, 1]
 PLACES = np.arange(512).reshape(SIZES)
-BY_HEAD = np.roll(PLACES, (-FIRST_Z, -FIRST_Y), (0, 3)).transpose(1, 2, 4, 0, 3).reshape(8, SLOTS)
+BY_HEAD = np.roll(PLACES, (-FIRST_Z, -FIRST_Y), (0, 3)).transpose(1, 2, 4, 3, 0).reshape(8, SLOTS)
 BY_X = PLACES.transpose(0, 2, 3, 1, 4).reshape(128, 4)[:, X_ORDER]
 BY_CORE = PLACES.transpose(0, 1, 3, 4, 2).reshape(256, 2)
 
@@ -39,8 +39,8 @@
 
 
 def token_of(row, xh, core, xl):
-    z = (row // 64 + FIRST_Z) % 8
-    y = (row // 8 + FIRST_Y) % 8
+    z = (row // 8 + FIRST_Z) % 8
+    y = (row // 64 + FIRST_Y) % 8
     return z * 512 + xh * 256 + core * 128 + y * 16 + xl * 8 + row % 8
 
 

time: 73 us -> 72.6 us (level)
  starting transfers between devices: 4.75 us -> 3.9 us
    ppermute x1, starting transfers between devices: 4.75 us -> 3.9 us  [body(): lax.ppermute(near, 'device', [(a, b) for a, b in BY_CORE.tolist()] + [(b,...]
where the time goes in v5:
time: 72.6 us; the launch traced here: 72.3 us
  blocking collectives  60.6 us (83%)
  Pallas kernels  5.52 us (8%)
  starting transfers between devices  3.9 us (5%)
  matrix products  1.31 us (2%)
  local copies, waits for them, and re-layouts  0.91 us (1%)
    all_to_all x3, blocking collectives, exchange(): lax.all_to_all(array, 'device', 0, 0, axis_index_groups=groups.tolist(),...  60.6 us
    pallas_call x2, Pallas kernels, attend(): pl.pallas_call(functools.partial(attend_kernel, its_core, bool(state)), o...  5.52 us
    ppermute x1, starting transfers between devices, body(): lax.ppermute(near, 'device', [(a, b) for a, b in BY_CORE.tolist()] + [(b,...  3.9 us
  transfers between devices with their start and end apart: 1, of which 0 were waited for; matrix products, arithmetic and copies ran while one was open for 0% of the time, Pallas kernels for 4%

profile of v5, /device:TPU:1, one launch (start us, length us, event | category | flops | bytes accessed | tf_op | source)
XLA Modules:
  0.0 72.3 jit_solution(2077766835761433692)
XLA Ops:
  0.0 1.3 %fusion.1 = bf16[3,48,8,128]{3,2,1,0:T(8,128)(2,1)S(1)} fusion(s32[6144]{0:T(1024)S(1)} %add_select_fusion, bf16[8,6144]{1,0:T(8,128)(2,1)} %param.7, bf16[8,6144]{1,0:T(8,128)(2,1)} %param.6, bf16[8,6144]{1,0:T(8,128)(2,1)} %param.5, s32[3,8,48]{2,1,0:T(8,128)} %param.8), kind=kOutput, calls=%fused_computation.3 | convolution fusion | flops 15633792 | bytes 619008 | tf_op jit(solution)/shard_map/dot_general | solution.py:138
  1.3 0.1 copy.11
  1.4 28.7 %all_to_all.15 = bf16[64,24,128]{2,1,0:T(8,128)(2,1)S(1)} all-to-all(bf16[64,24,128]{2,1,0:T(8,128)(2,1)S(1)} %pad.4), channel_id=1, replica_groups={{328,392,456,8,72,136,200,264,330,394,458,10,74,138,202,266,332,396,460..., dimensions={0} | all-to-all | bytes 786432 | tf_op jit(solution)/shard_map/all_to_all | solution.py:145
  30.1 0.1 broadcast_in_dim.10
  30.3 0.0 copy-start
  30.3 16.3 %all_to_all.16.kv_ref = bf16[4,2,512,128]{3,2,1,0:T(8,128)(2,1)S(1)} all-to-all(bf16[4,2,512,128]{3,2,1,0:T(8,128)(2,1)S(1)} %broadcast_in_dim.10), channel_id=1, replica_groups={{32,0,33,1},{34,2,35,3},{36,4,37,5},{38,6,39,7},{40,8,41,9},{42,10,43,1..., dimensions={0} | all-to-all | bytes 2097152 | tf_op jit(solution)/shard_map/all_to_all | solution.py:145
  46.5 3.9 %collective-permute-start = (bf16[4,2,512,128]{3,2,1,0:T(8,128)(2,1)S(1)}, bf16[4,2,512,128]{3,2,1,0:T(8,128)(2,1)S(1)}, u32[]{:S(2)}, u32[]{:S(2)}) collective-permute-start(bf16[4,2,512,128]{3,2,1,0:T(8,128)(2,1)S(1)} %all_to_all.16.kv_ref), channel_id=1, source_target_pairs={{0,16},{1,17},{2,18},{3,19},{4,20},{5,21},{6,22},{7,23},{8,24},{9,... | collective-permute-start | bytes 3145736 | tf_op jit(solution)/shard_map/ppermute | solution.py:155
  50.5 0.0 copy-done
  50.5 2.7 %shard_map.55 = (f32[512,128]{1,0:T(8,128)S(1)}, f32[512,128]{1,0:T(8,128)S(1)}, f32[512,128]{1,0:T(8,128)S(1)}) custom-call(s32[4]{0:T(128)S(1)} %copy-done, bf16[512,128]{1,0:T(8,128)(2,1)S(1)} %slice_bitcast_fusion.1.q_ref, bf16[4,2,512,128]{3,2,1,0:T(8,128)(2,1)S(1)} %all_to_all.16.kv_ref), custom_call_target="tpu_custom_call" | custom-call | flops 536870912 | bytes 1048576 | tf_op jit(solution)/shard_map/pallas_call | solution.py:121
  53.1 0.0 collective-permute-done.kv_ref
  53.1 2.9 %shard_map.56 = bf16[512,128]{1,0:T(8,128)(2,1)S(1)} custom-call(s32[4]{0:T(128)S(1)} %copy-done, bf16[512,128]{1,0:T(8,128)(2,1)S(1)} %slice_bitcast_fusion.1.q_ref, bf16[4,2,512,128]{3,2,1,0:T(8,128)(2,1)S(1)} %collective-permute-done.kv_ref, f32[512,128]{1,0:T(8,128)S(1)} %get-tuple-element.8.refs_0_, f32[512,128]{1,0:T(8,128)S(1)} %get-tuple-element.9.refs_1_, ...), custom_call_target="tpu_custom_call" | custom-call | flops 536870912 | bytes 1048576 | tf_op jit(solution)/shard_map/pallas_call | solution.py:121
  56.0 15.6 %all_to_all.17 = bf16[64,8,128]{2,1,0:T(8,128)(2,1)S(1)} all-to-all(bf16[64,8,128]{2,1,0:T(8,128)(2,1)S(1)} %bitcast.25), channel_id=1, replica_groups={{328,392,456,8,72,136,200,264,330,394,458,10,74,138,202,266,332,396,460..., dimensions={0} | all-to-all | bytes 262144 | tf_op jit(solution)/shard_map/all_to_all | solution.py:145
  71.7 0.6 slice_bitcast_fusion.2
  (4 shorter events, 0.1 us)
Async XLA Ops:
  30.3 20.2 %copy-start = (s32[4]{0:T(128)S(1)}, s32[4]{0:T(128)}, u32[]{:S(2)}) copy-start(s32[4]{0:T(128)} %length_ref.3) | copy-start | bytes 52
  46.5 6.6 %collective-permute-start = (bf16[4,2,512,128]{3,2,1,0:T(8,128)(2,1)S(1)}, bf16[4,2,512,128]{3,2,1,0:T(8,128)(2,1)S(1)}, u32[]{:S(2)}, u32[]{:S(2)}) collective-permute-start(bf16[4,2,512,128]{3,2,1,0:T(8,128)(2,1)S(1)} %all_to_all.16.kv_ref), channel_id=1, source_target_pairs={{0,16},{1,17},{2,18},{3,19},{4,20},{5,21},{6,22},{7,23},{8,24},{9,... | collective-permute-start | bytes 3145736 | tf_op jit(solution)/shard_map/ppermute | solution.py:155

commit v6 on v5

--- a/solution.py
+++ b/solution.py
@@ -30,18 +30,17 @@
 
 
 def clip_of(length_ref, token):
-    end = jnp.int32(0)
-    clip = jnp.zeros_like(token)
-    for i in range(4):
-        end = end + length_ref[i]
-        clip = clip + (end <= token).astype(jnp.int32)
-    return clip
+    first = length_ref[0]
+    second = first + length_ref[1]
+    third = second + length_ref[2]
+    ends = (token >= first, token >= second, token >= third)
+    return sum(end.astype(jnp.int32) for end in ends)
 
 
 def token_of(row, xh, core, xl):
-    z = (row // 8 + FIRST_Z) % 8
-    y = (row // 64 + FIRST_Y) % 8
-    return z * 512 + xh * 256 + core * 128 + y * 16 + xl * 8 + row % 8
+    z = ((row >> 3) + FIRST_Z) & 7
+    y = ((row >> 6) + FIRST_Y) & 7
+    return (z << 9) + (y << 4) + (row & 7) + (xh * 256 + core * 128 + xl * 8)
 
 
 QB = 256

time: 72.6 us -> 72.1 us (level)
  transfers between devices with their start and end apart: 1 -> 1, of which waited for: 0 -> 0; matrix products, arithmetic and copies ran while one was open for 0% -> 0% of each run, Pallas kernels for 4% -> 3%
where the time goes in v6:
time: 72.1 us; the launch traced here: 71.9 us
  blocking collectives  60.6 us (84%)
  Pallas kernels  5.1 us (7%)
  starting transfers between devices  3.9 us (5%)
  matrix products  1.31 us (2%)
  local copies, waits for them, and re-layouts  0.91 us (1%)
    all_to_all x3, blocking collectives, exchange(): lax.all_to_all(array, 'device', 0, 0, axis_index_groups=groups.tolist(),...  60.6 us
    pallas_call x2, Pallas kernels, attend(): pl.pallas_call(functools.partial(attend_kernel, its_core, bool(state)), o...  5.1 us
    ppermute x1, starting transfers between devices, body(): lax.ppermute(near, 'device', [(a, b) for a, b in BY_CORE.tolist()] + [(b,...  3.9 us
  transfers between devices with their start and end apart: 1, of which 0 were waited for; matrix products, arithmetic and copies ran while one was open for 0% of the time, Pallas kernels for 3%

profile of v6, /device:TPU:1, one launch (start us, length us, event | category | flops | bytes accessed | tf_op | source)
XLA Modules:
  0.0 71.9 jit_solution(13900489611642958075)
XLA Ops:
  0.0 1.3 %fusion.1 = bf16[3,48,8,128]{3,2,1,0:T(8,128)(2,1)S(1)} fusion(s32[6144]{0:T(1024)S(1)} %add_select_fusion, bf16[8,6144]{1,0:T(8,128)(2,1)} %param.7, bf16[8,6144]{1,0:T(8,128)(2,1)} %param.6, bf16[8,6144]{1,0:T(8,128)(2,1)} %param.5, s32[3,8,48]{2,1,0:T(8,128)} %param.8), kind=kOutput, calls=%fused_computation.3 | convolution fusion | flops 15633792 | bytes 619008 | tf_op jit(solution)/shard_map/dot_general | solution.py:137
  1.3 0.1 copy.11
  1.4 28.7 %all_to_all.15 = bf16[64,24,128]{2,1,0:T(8,128)(2,1)S(1)} all-to-all(bf16[64,24,128]{2,1,0:T(8,128)(2,1)S(1)} %pad.4), channel_id=1, replica_groups={{328,392,456,8,72,136,200,264,330,394,458,10,74,138,202,266,332,396,460..., dimensions={0} | all-to-all | bytes 786432 | tf_op jit(solution)/shard_map/all_to_all | solution.py:144
  30.1 0.1 broadcast_in_dim.10
  30.3 0.0 copy-start
  30.3 16.3 %all_to_all.16.kv_ref = bf16[4,2,512,128]{3,2,1,0:T(8,128)(2,1)S(1)} all-to-all(bf16[4,2,512,128]{3,2,1,0:T(8,128)(2,1)S(1)} %broadcast_in_dim.10), channel_id=1, replica_groups={{32,0,33,1},{34,2,35,3},{36,4,37,5},{38,6,39,7},{40,8,41,9},{42,10,43,1..., dimensions={0} | all-to-all | bytes 2097152 | tf_op jit(solution)/shard_map/all_to_all | solution.py:144
  46.5 3.9 %collective-permute-start = (bf16[4,2,512,128]{3,2,1,0:T(8,128)(2,1)S(1)}, bf16[4,2,512,128]{3,2,1,0:T(8,128)(2,1)S(1)}, u32[]{:S(2)}, u32[]{:S(2)}) collective-permute-start(bf16[4,2,512,128]{3,2,1,0:T(8,128)(2,1)S(1)} %all_to_all.16.kv_ref), channel_id=1, source_target_pairs={{0,16},{1,17},{2,18},{3,19},{4,20},{5,21},{6,22},{7,23},{8,24},{9,... | collective-permute-start | bytes 3145736 | tf_op jit(solution)/shard_map/ppermute | solution.py:154
  50.5 0.0 copy-done
  50.5 2.5 %shard_map.55 = (f32[512,128]{1,0:T(8,128)S(1)}, f32[512,128]{1,0:T(8,128)S(1)}, f32[512,128]{1,0:T(8,128)S(1)}) custom-call(s32[4]{0:T(128)S(1)} %copy-done, bf16[512,128]{1,0:T(8,128)(2,1)S(1)} %slice_bitcast_fusion.1.q_ref, bf16[4,2,512,128]{3,2,1,0:T(8,128)(2,1)S(1)} %all_to_all.16.kv_ref), custom_call_target="tpu_custom_call" | custom-call | flops 536870912 | bytes 1048576 | tf_op jit(solution)/shard_map/pallas_call | solution.py:120
  52.9 0.0 collective-permute-done.kv_ref
  52.9 2.6 %shard_map.56 = bf16[512,128]{1,0:T(8,128)(2,1)S(1)} custom-call(s32[4]{0:T(128)S(1)} %copy-done, bf16[512,128]{1,0:T(8,128)(2,1)S(1)} %slice_bitcast_fusion.1.q_ref, bf16[4,2,512,128]{3,2,1,0:T(8,128)(2,1)S(1)} %collective-permute-done.kv_ref, f32[512,128]{1,0:T(8,128)S(1)} %get-tuple-element.8.refs_0_, f32[512,128]{1,0:T(8,128)S(1)} %get-tuple-element.9.refs_1_, ...), custom_call_target="tpu_custom_call" | custom-call | flops 536870912 | bytes 1048576 | tf_op jit(solution)/shard_map/pallas_call | solution.py:120
  55.6 15.6 %all_to_all.17 = bf16[64,8,128]{2,1,0:T(8,128)(2,1)S(1)} all-to-all(bf16[64,8,128]{2,1,0:T(8,128)(2,1)S(1)} %bitcast.25), channel_id=1, replica_groups={{328,392,456,8,72,136,200,264,330,394,458,10,74,138,202,266,332,396,460..., dimensions={0} | all-to-all | bytes 262144 | tf_op jit(solution)/shard_map/all_to_all | solution.py:144
  71.2 0.6 slice_bitcast_fusion.2
  (4 shorter events, 0.1 us)
Async XLA Ops:
  30.3 20.2 %copy-start = (s32[4]{0:T(128)S(1)}, s32[4]{0:T(128)}, u32[]{:S(2)}) copy-start(s32[4]{0:T(128)} %length_ref.3) | copy-start | bytes 52
  46.5 6.4 %collective-permute-start = (bf16[4,2,512,128]{3,2,1,0:T(8,128)(2,1)S(1)}, bf16[4,2,512,128]{3,2,1,0:T(8,128)(2,1)S(1)}, u32[]{:S(2)}, u32[]{:S(2)}) collective-permute-start(bf16[4,2,512,128]{3,2,1,0:T(8,128)(2,1)S(1)} %all_to_all.16.kv_ref), channel_id=1, source_target_pairs={{0,16},{1,17},{2,18},{3,19},{4,20},{5,21},{6,22},{7,23},{8,24},{9,... | collective-permute-start | bytes 3145736 | tf_op jit(solution)/shard_map/ppermute | solution.py:154

commit v7 on v6

--- a/solution.py
+++ b/solution.py
@@ -85,11 +85,7 @@
     for block in range(blocks):
         highest = jnp.max(top, axis=1, keepdims=True)
         shift = highest * factor
-        if carried:
-            old = jnp.exp2(top_ref[rows(block), :] * factor - shift)
-            total, numerator = sum_ref[rows(block), :] * old, acc_ref[rows(block), :] * old
-        else:
-            total = numerator = jnp.zeros((QB, HEAD), jnp.float32)
+        total = numerator = jnp.zeros((QB, HEAD), jnp.float32)
         if block + 1 < blocks:
             query, query_clip, top = begin(block + 1)
         for x in range(4):
@@ -102,6 +98,9 @@
                 weights.astype(jnp.bfloat16), kv_ref[x, 1], preferred_element_type=jnp.float32
             )
         if carried:
+            old = jnp.exp2(top_ref[rows(block), :] * factor - shift)
+            total = total + sum_ref[rows(block), :] * old
+            numerator = numerator + acc_ref[rows(block), :] * old
             out_ref[rows(block), :] = (
                 numerator / jnp.sum(total, axis=1, keepdims=True)
             ).astype(jnp.bfloat16)
@@ -132,12 +131,13 @@
 
 def pack(q_payload, k_payload, v_payload, exponents):
     scale = jnp.exp2(exponents.astype(jnp.float32)).astype(jnp.bfloat16).reshape(3 * ROWS, HEADS)
-    lane_head = jnp.arange(HEADS * HEAD) // HEAD
+    lane_head = jnp.arange(SLOTS * HEAD) // HEAD
     spread = (jnp.arange(HEADS)[:, None] == lane_head[None, :]).astype(jnp.bfloat16)
     scale = jnp.dot(scale, spread, preferred_element_type=jnp.float32)
     payload = jnp.concatenate([q_payload, k_payload, v_payload]).astype(jnp.float32)
-    packed = (payload * scale).astype(jnp.bfloat16).reshape(3 * ROWS, HEADS, HEAD)
-    return jnp.pad(packed.transpose(1, 0, 2), ((0, SLOTS - HEADS), (0, 0), (0, 0)))
+    payload = jnp.pad(payload, ((0, 0), (0, (SLOTS - HEADS) * HEAD)))
+    packed = (payload * scale).astype(jnp.bfloat16).reshape(3 * ROWS, SLOTS, HEAD)
+    return packed.transpose(1, 0, 2)
 
 
 def exchange(array, groups):

time: 72.1 us -> 72.2 us (level)
  no operation moved by 1% of the time
where the time goes in v7:
time: 72.2 us; the launch traced here: 71.9 us
  blocking collectives  60.6 us (84%)
  Pallas kernels  5.12 us (7%)
  starting transfers between devices  3.9 us (5%)
  matrix products  1.38 us (2%)
  local copies, waits for them, and re-layouts  0.89 us (1%)
    all_to_all x3, blocking collectives, exchange(): lax.all_to_all(array, 'device', 0, 0, axis_index_groups=groups.tolist(),...  60.6 us
    pallas_call x2, Pallas kernels, attend(): pl.pallas_call(functools.partial(attend_kernel, its_core, bool(state)), o...  5.12 us
    ppermute x1, starting transfers between devices, body(): lax.ppermute(near, 'device', [(a, b) for a, b in BY_CORE.tolist()] + [(b,...  3.9 us
  transfers between devices with their start and end apart: 1, of which 0 were waited for; matrix products, arithmetic and copies ran while one was open for 0% of the time, Pallas kernels for 3%

profile of v7, /device:TPU:1, one launch (start us, length us, event | category | flops | bytes accessed | tf_op | source)
XLA Modules:
  0.0 71.9 jit_solution(14652386809213190710)
XLA Ops:
  0.0 1.4 %fusion.1 = bf16[3,64,8,128]{3,2,1,0:T(8,128)(2,1)S(1)} fusion(s32[8192]{0:T(1024)S(1)} %add_select_fusion, bf16[8,6144]{1,0:T(8,128)(2,1)} %param.7, bf16[8,6144]{1,0:T(8,128)(2,1)} %param.6, bf16[8,6144]{1,0:T(8,128)(2,1)} %param.5, s32[3,8,48]{2,1,0:T(8,128)} %param.8), kind=kOutput, calls=%fused_computation.3 | convolution fusion | flops 21630336 | bytes 725504 | tf_op jit(solution)/shard_map/dot_general | solution.py:136
  1.4 0.1 copy.11
  1.5 28.7 %all_to_all.15 = bf16[64,24,128]{2,1,0:T(8,128)(2,1)S(1)} all-to-all(bf16[64,24,128]{2,1,0:T(8,128)(2,1)S(1)} %bitcast.26), channel_id=1, replica_groups={{328,392,456,8,72,136,200,264,330,394,458,10,74,138,202,266,332,396,460..., dimensions={0} | all-to-all | bytes 786432 | tf_op jit(solution)/shard_map/all_to_all | solution.py:144
  30.2 0.1 broadcast_in_dim.10
  30.3 0.0 copy-start
  30.3 16.3 %all_to_all.16.kv_ref = bf16[4,2,512,128]{3,2,1,0:T(8,128)(2,1)S(1)} all-to-all(bf16[4,2,512,128]{3,2,1,0:T(8,128)(2,1)S(1)} %broadcast_in_dim.10), channel_id=1, replica_groups={{32,0,33,1},{34,2,35,3},{36,4,37,5},{38,6,39,7},{40,8,41,9},{42,10,43,1..., dimensions={0} | all-to-all | bytes 2097152 | tf_op jit(solution)/shard_map/all_to_all | solution.py:144
  46.6 3.9 %collective-permute-start = (bf16[4,2,512,128]{3,2,1,0:T(8,128)(2,1)S(1)}, bf16[4,2,512,128]{3,2,1,0:T(8,128)(2,1)S(1)}, u32[]{:S(2)}, u32[]{:S(2)}) collective-permute-start(bf16[4,2,512,128]{3,2,1,0:T(8,128)(2,1)S(1)} %all_to_all.16.kv_ref), channel_id=1, source_target_pairs={{0,16},{1,17},{2,18},{3,19},{4,20},{5,21},{6,22},{7,23},{8,24},{9,... | collective-permute-start | bytes 3145736 | tf_op jit(solution)/shard_map/ppermute | solution.py:154
  50.5 0.0 copy-done
  50.5 2.5 %shard_map.55 = (f32[512,128]{1,0:T(8,128)S(1)}, f32[512,128]{1,0:T(8,128)S(1)}, f32[512,128]{1,0:T(8,128)S(1)}) custom-call(s32[4]{0:T(128)S(1)} %copy-done, bf16[512,128]{1,0:T(8,128)(2,1)S(1)} %slice_bitcast_fusion.1.q_ref, bf16[4,2,512,128]{3,2,1,0:T(8,128)(2,1)S(1)} %all_to_all.16.kv_ref), custom_call_target="tpu_custom_call" | custom-call | flops 536870912 | bytes 1048576 | tf_op jit(solution)/shard_map/pallas_call | solution.py:119
  53.0 0.0 collective-permute-done.kv_ref
  53.0 2.7 %shard_map.56 = bf16[512,128]{1,0:T(8,128)(2,1)S(1)} custom-call(s32[4]{0:T(128)S(1)} %copy-done, bf16[512,128]{1,0:T(8,128)(2,1)S(1)} %slice_bitcast_fusion.1.q_ref, bf16[4,2,512,128]{3,2,1,0:T(8,128)(2,1)S(1)} %collective-permute-done.kv_ref, f32[512,128]{1,0:T(8,128)S(1)} %get-tuple-element.8.refs_0_, f32[512,128]{1,0:T(8,128)S(1)} %get-tuple-element.9.refs_1_, ...), custom_call_target="tpu_custom_call" | custom-call | flops 536870912 | bytes 1048576 | tf_op jit(solution)/shard_map/pallas_call | solution.py:119
  55.6 15.6 %all_to_all.17 = bf16[64,8,128]{2,1,0:T(8,128)(2,1)S(1)} all-to-all(bf16[64,8,128]{2,1,0:T(8,128)(2,1)S(1)} %bitcast.25), channel_id=1, replica_groups={{328,392,456,8,72,136,200,264,330,394,458,10,74,138,202,266,332,396,460..., dimensions={0} | all-to-all | bytes 262144 | tf_op jit(solution)/shard_map/all_to_all | solution.py:144
  71.3 0.6 slice_bitcast_fusion.2
  (3 shorter events, 0.0 us)
Async XLA Ops:
  30.3 20.2 %copy-start = (s32[4]{0:T(128)S(1)}, s32[4]{0:T(128)}, u32[]{:S(2)}) copy-start(s32[4]{0:T(128)} %length_ref.3) | copy-start | bytes 52
  46.6 6.4 %collective-permute-start = (bf16[4,2,512,128]{3,2,1,0:T(8,128)(2,1)S(1)}, bf16[4,2,512,128]{3,2,1,0:T(8,128)(2,1)S(1)}, u32[]{:S(2)}, u32[]{:S(2)}) collective-permute-start(bf16[4,2,512,128]{3,2,1,0:T(8,128)(2,1)S(1)} %all_to_all.16.kv_ref), channel_id=1, source_target_pairs={{0,16},{1,17},{2,18},{3,19},{4,20},{5,21},{6,22},{7,23},{8,24},{9,... | collective-permute-start | bytes 3145736 | tf_op jit(solution)/shard_map/ppermute | solution.py:154

commit v8 on v7

--- a/solution.py
+++ b/solution.py
@@ -150,7 +150,7 @@
     query = mine[:, :ROWS].reshape(OWN, HEAD)
     own = mine[:, ROWS:].reshape(1, SLOTS, 2, ROWS, HEAD).transpose(0, 2, 1, 3, 4)
     own = own.reshape(1, 2, OWN, HEAD)
-    near = exchange(jnp.broadcast_to(own, (4, 2, OWN, HEAD)), BY_X)
+    near = exchange(jnp.concatenate([own] * 4), BY_X)
     far = lax.ppermute(near, "device", [(a, b) for a, b in BY_CORE.tolist()] + [(b, a) for a, b in BY_CORE.tolist()])
     state = attend(True, lengths, query, near)
     attended = attend(False, lengths, query, far, state)

time: 72.2 us -> 72.2 us (level)
  no operation moved by 1% of the time
where the time goes in v8:
time: 72.2 us; the launch traced here: 71.9 us
  blocking collectives  60.6 us (84%)
  Pallas kernels  5.12 us (7%)
  starting transfers between devices  3.9 us (5%)
  matrix products  1.38 us (2%)
  local copies, waits for them, and re-layouts  0.89 us (1%)
    all_to_all x3, blocking collectives, exchange(): lax.all_to_all(array, 'device', 0, 0, axis_index_groups=groups.tolist(),...  60.6 us
    pallas_call x2, Pallas kernels, attend(): pl.pallas_call(functools.partial(attend_kernel, its_core, bool(state)), o...  5.12 us
    ppermute x1, starting transfers between devices, body(): lax.ppermute(near, 'device', [(a, b) for a, b in BY_CORE.tolist()] + [(b,...  3.9 us
  transfers between devices with their start and end apart: 1, of which 0 were waited for; matrix products, arithmetic and copies ran while one was open for 0% of the time, Pallas kernels for 3%

profile of v8, /device:TPU:1, one launch (start us, length us, event | category | flops | bytes accessed | tf_op | source)
XLA Modules:
  0.0 71.9 jit_solution(14652386809213190710)
XLA Ops:
  0.0 1.4 %fusion.1 = bf16[3,64,8,128]{3,2,1,0:T(8,128)(2,1)S(1)} fusion(s32[8192]{0:T(1024)S(1)} %add_select_fusion, bf16[8,6144]{1,0:T(8,128)(2,1)} %param.7, bf16[8,6144]{1,0:T(8,128)(2,1)} %param.6, bf16[8,6144]{1,0:T(8,128)(2,1)} %param.5, s32[3,8,48]{2,1,0:T(8,128)} %param.8), kind=kOutput, calls=%fused_computation.3 | convolution fusion | flops 21630336 | bytes 725504 | tf_op jit(solution)/shard_map/dot_general | solution.py:136
  1.4 0.1 copy.11
  1.5 28.7 %all_to_all.15 = bf16[64,24,128]{2,1,0:T(8,128)(2,1)S(1)} all-to-all(bf16[64,24,128]{2,1,0:T(8,128)(2,1)S(1)} %bitcast.26), channel_id=1, replica_groups={{328,392,456,8,72,136,200,264,330,394,458,10,74,138,202,266,332,396,460..., dimensions={0} | all-to-all | bytes 786432 | tf_op jit(solution)/shard_map/all_to_all | solution.py:144
  30.2 0.1 concatenate.7
  30.3 0.0 copy-start
  30.3 16.3 %all_to_all.16.kv_ref = bf16[4,2,512,128]{3,2,1,0:T(8,128)(2,1)S(1)} all-to-all(bf16[4,2,512,128]{3,2,1,0:T(8,128)(2,1)S(1)} %concatenate.7), channel_id=1, replica_groups={{32,0,33,1},{34,2,35,3},{36,4,37,5},{38,6,39,7},{40,8,41,9},{42,10,43,1..., dimensions={0} | all-to-all | bytes 2097152 | tf_op jit(solution)/shard_map/all_to_all | solution.py:144
  46.6 3.9 %collective-permute-start = (bf16[4,2,512,128]{3,2,1,0:T(8,128)(2,1)S(1)}, bf16[4,2,512,128]{3,2,1,0:T(8,128)(2,1)S(1)}, u32[]{:S(2)}, u32[]{:S(2)}) collective-permute-start(bf16[4,2,512,128]{3,2,1,0:T(8,128)(2,1)S(1)} %all_to_all.16.kv_ref), channel_id=1, source_target_pairs={{0,16},{1,17},{2,18},{3,19},{4,20},{5,21},{6,22},{7,23},{8,24},{9,... | collective-permute-start | bytes 3145736 | tf_op jit(solution)/shard_map/ppermute | solution.py:154
  50.5 0.0 copy-done
  50.5 2.5 %shard_map.55 = (f32[512,128]{1,0:T(8,128)S(1)}, f32[512,128]{1,0:T(8,128)S(1)}, f32[512,128]{1,0:T(8,128)S(1)}) custom-call(s32[4]{0:T(128)S(1)} %copy-done, bf16[512,128]{1,0:T(8,128)(2,1)S(1)} %slice_bitcast_fusion.1.q_ref, bf16[4,2,512,128]{3,2,1,0:T(8,128)(2,1)S(1)} %all_to_all.16.kv_ref), custom_call_target="tpu_custom_call" | custom-call | flops 536870912 | bytes 1048576 | tf_op jit(solution)/shard_map/pallas_call | solution.py:119
  53.0 0.0 collective-permute-done.kv_ref
  53.0 2.7 %shard_map.56 = bf16[512,128]{1,0:T(8,128)(2,1)S(1)} custom-call(s32[4]{0:T(128)S(1)} %copy-done, bf16[512,128]{1,0:T(8,128)(2,1)S(1)} %slice_bitcast_fusion.1.q_ref, bf16[4,2,512,128]{3,2,1,0:T(8,128)(2,1)S(1)} %collective-permute-done.kv_ref, f32[512,128]{1,0:T(8,128)S(1)} %get-tuple-element.8.refs_0_, f32[512,128]{1,0:T(8,128)S(1)} %get-tuple-element.9.refs_1_, ...), custom_call_target="tpu_custom_call" | custom-call | flops 536870912 | bytes 1048576 | tf_op jit(solution)/shard_map/pallas_call | solution.py:119
  55.6 15.6 %all_to_all.17 = bf16[64,8,128]{2,1,0:T(8,128)(2,1)S(1)} all-to-all(bf16[64,8,128]{2,1,0:T(8,128)(2,1)S(1)} %bitcast.25), channel_id=1, replica_groups={{328,392,456,8,72,136,200,264,330,394,458,10,74,138,202,266,332,396,460..., dimensions={0} | all-to-all | bytes 262144 | tf_op jit(solution)/shard_map/all_to_all | solution.py:144
  71.3 0.6 slice_bitcast_fusion.2
  (3 shorter events, 0.0 us)
Async XLA Ops:
  30.3 20.2 %copy-start = (s32[4]{0:T(128)S(1)}, s32[4]{0:T(128)}, u32[]{:S(2)}) copy-start(s32[4]{0:T(128)} %length_ref.3) | copy-start | bytes 52
  46.6 6.4 %collective-permute-start = (bf16[4,2,512,128]{3,2,1,0:T(8,128)(2,1)S(1)}, bf16[4,2,512,128]{3,2,1,0:T(8,128)(2,1)S(1)}, u32[]{:S(2)}, u32[]{:S(2)}) collective-permute-start(bf16[4,2,512,128]{3,2,1,0:T(8,128)(2,1)S(1)} %all_to_all.16.kv_ref), channel_id=1, source_target_pairs={{0,16},{1,17},{2,18},{3,19},{4,20},{5,21},{6,22},{7,23},{8,24},{9,... | collective-permute-start | bytes 3145736 | tf_op jit(solution)/shard_map/ppermute | solution.py:154

commit v9 on v8

--- a/solution.py
+++ b/solution.py
@@ -17,7 +17,7 @@
 ROWS = 8
 OWN = SLOTS * ROWS
 FIRST_Z, FIRST_Y = 5, 4
-X_ORDER = [2, 0, 3, 1]
+X_ORDER = [2, 1, 3, 0]
 PLACES = np.arange(512).reshape(SIZES)
 BY_HEAD = np.roll(PLACES, (-FIRST_Z, -FIRST_Y), (0, 3)).transpose(1, 2, 4, 3, 0).reshape(8, SLOTS)
 BY_X = PLACES.transpose(0, 2, 3, 1, 4).reshape(128, 4)[:, X_ORDER]
@@ -134,9 +134,9 @@
     lane_head = jnp.arange(SLOTS * HEAD) // HEAD
     spread = (jnp.arange(HEADS)[:, None] == lane_head[None, :]).astype(jnp.bfloat16)
     scale = jnp.dot(scale, spread, preferred_element_type=jnp.float32)
-    payload = jnp.concatenate([q_payload, k_payload, v_payload]).astype(jnp.float32)
+    payload = jnp.concatenate([q_payload, k_payload, v_payload])
     payload = jnp.pad(payload, ((0, 0), (0, (SLOTS - HEADS) * HEAD)))
-    packed = (payload * scale).astype(jnp.bfloat16).reshape(3 * ROWS, SLOTS, HEAD)
+    packed = (payload * scale.astype(jnp.bfloat16)).reshape(3 * ROWS, SLOTS, HEAD)
     return packed.transpose(1, 0, 2)
 
 

time: 72.2 us -> 72.2 us (level)
  no operation moved by 1% of the time
where the time goes in v9:
time: 72.2 us; the launch traced here: 71.9 us
  blocking collectives  60.6 us (84%)
  Pallas kernels  5.11 us (7%)
  starting transfers between devices  3.9 us (5%)
  matrix products  1.38 us (2%)
  local copies, waits for them, and re-layouts  0.89 us (1%)
    all_to_all x3, blocking collectives, exchange(): lax.all_to_all(array, 'device', 0, 0, axis_index_groups=groups.tolist(),...  60.6 us
    pallas_call x2, Pallas kernels, attend(): pl.pallas_call(functools.partial(attend_kernel, its_core, bool(state)), o...  5.11 us
    ppermute x1, starting transfers between devices, body(): lax.ppermute(near, 'device', [(a, b) for a, b in BY_CORE.tolist()] + [(b,...  3.9 us
  transfers between devices with their start and end apart: 1, of which 0 were waited for; matrix products, arithmetic and copies ran while one was open for 0% of the time, Pallas kernels for 3%

profile of v9, /device:TPU:1, one launch (start us, length us, event | category | flops | bytes accessed | tf_op | source)
XLA Modules:
  0.0 71.9 jit_solution(2610998193590181259)
XLA Ops:
  0.0 1.4 %fusion.1 = bf16[3,64,8,128]{3,2,1,0:T(8,128)(2,1)S(1)} fusion(s32[8192]{0:T(1024)S(1)} %add_select_fusion, bf16[8,6144]{1,0:T(8,128)(2,1)} %param.7, bf16[8,6144]{1,0:T(8,128)(2,1)} %param.6, bf16[8,6144]{1,0:T(8,128)(2,1)} %param.5, s32[3,8,48]{2,1,0:T(8,128)} %param.8), kind=kOutput, calls=%fused_computation.3 | convolution fusion | flops 21826944 | bytes 725504 | tf_op jit(solution)/shard_map/dot_general | solution.py:136
  1.4 0.1 copy.11
  1.5 28.7 %all_to_all.15 = bf16[64,24,128]{2,1,0:T(8,128)(2,1)S(1)} all-to-all(bf16[64,24,128]{2,1,0:T(8,128)(2,1)S(1)} %bitcast.26), channel_id=1, replica_groups={{328,392,456,8,72,136,200,264,330,394,458,10,74,138,202,266,332,396,460..., dimensions={0} | all-to-all | bytes 786432 | tf_op jit(solution)/shard_map/all_to_all | solution.py:144
  30.2 0.1 concatenate.7
  30.3 0.0 copy-start
  30.3 16.3 %all_to_all.16.kv_ref = bf16[4,2,512,128]{3,2,1,0:T(8,128)(2,1)S(1)} all-to-all(bf16[4,2,512,128]{3,2,1,0:T(8,128)(2,1)S(1)} %concatenate.7), channel_id=1, replica_groups={{32,1,33,0},{34,3,35,2},{36,5,37,4},{38,7,39,6},{40,9,41,8},{42,11,43,1..., dimensions={0} | all-to-all | bytes 2097152 | tf_op jit(solution)/shard_map/all_to_all | solution.py:144
  46.6 3.9 %collective-permute-start = (bf16[4,2,512,128]{3,2,1,0:T(8,128)(2,1)S(1)}, bf16[4,2,512,128]{3,2,1,0:T(8,128)(2,1)S(1)}, u32[]{:S(2)}, u32[]{:S(2)}) collective-permute-start(bf16[4,2,512,128]{3,2,1,0:T(8,128)(2,1)S(1)} %all_to_all.16.kv_ref), channel_id=1, source_target_pairs={{0,16},{1,17},{2,18},{3,19},{4,20},{5,21},{6,22},{7,23},{8,24},{9,... | collective-permute-start | bytes 3145736 | tf_op jit(solution)/shard_map/ppermute | solution.py:154
  50.5 0.0 copy-done
  50.5 2.5 %shard_map.55 = (f32[512,128]{1,0:T(8,128)S(1)}, f32[512,128]{1,0:T(8,128)S(1)}, f32[512,128]{1,0:T(8,128)S(1)}) custom-call(s32[4]{0:T(128)S(1)} %copy-done, bf16[512,128]{1,0:T(8,128)(2,1)S(1)} %slice_bitcast_fusion.1.q_ref, bf16[4,2,512,128]{3,2,1,0:T(8,128)(2,1)S(1)} %all_to_all.16.kv_ref), custom_call_target="tpu_custom_call" | custom-call | flops 536870912 | bytes 1048576 | tf_op jit(solution)/shard_map/pallas_call | solution.py:119
  53.0 0.0 collective-permute-done.kv_ref
  53.0 2.7 %shard_map.56 = bf16[512,128]{1,0:T(8,128)(2,1)S(1)} custom-call(s32[4]{0:T(128)S(1)} %copy-done, bf16[512,128]{1,0:T(8,128)(2,1)S(1)} %slice_bitcast_fusion.1.q_ref, bf16[4,2,512,128]{3,2,1,0:T(8,128)(2,1)S(1)} %collective-permute-done.kv_ref, f32[512,128]{1,0:T(8,128)S(1)} %get-tuple-element.8.refs_0_, f32[512,128]{1,0:T(8,128)S(1)} %get-tuple-element.9.refs_1_, ...), custom_call_target="tpu_custom_call" | custom-call | flops 536870912 | bytes 1048576 | tf_op jit(solution)/shard_map/pallas_call | solution.py:119
  55.7 15.6 %all_to_all.17 = bf16[64,8,128]{2,1,0:T(8,128)(2,1)S(1)} all-to-all(bf16[64,8,128]{2,1,0:T(8,128)(2,1)S(1)} %bitcast.25), channel_id=1, replica_groups={{328,392,456,8,72,136,200,264,330,394,458,10,74,138,202,266,332,396,460..., dimensions={0} | all-to-all | bytes 262144 | tf_op jit(solution)/shard_map/all_to_all | solution.py:144
  71.3 0.6 slice_bitcast_fusion.2
  (3 shorter events, 0.0 us)
Async XLA Ops:
  30.3 20.2 %copy-start = (s32[4]{0:T(128)S(1)}, s32[4]{0:T(128)}, u32[]{:S(2)}) copy-start(s32[4]{0:T(128)} %length_ref.3) | copy-start | bytes 52
  46.6 6.4 %collective-permute-start = (bf16[4,2,512,128]{3,2,1,0:T(8,128)(2,1)S(1)}, bf16[4,2,512,128]{3,2,1,0:T(8,128)(2,1)S(1)}, u32[]{:S(2)}, u32[]{:S(2)}) collective-permute-start(bf16[4,2,512,128]{3,2,1,0:T(8,128)(2,1)S(1)} %all_to_all.16.kv_ref), channel_id=1, source_target_pairs={{0,16},{1,17},{2,18},{3,19},{4,20},{5,21},{6,22},{7,23},{8,24},{9,... | collective-permute-start | bytes 3145736 | tf_op jit(solution)/shard_map/ppermute | solution.py:154

commit v10 on v9

--- a/solution.py
+++ b/solution.py
@@ -89,11 +89,13 @@
         if block + 1 < blocks:
             query, query_clip, top = begin(block + 1)
         for x in range(4):
-            if block + 1 < blocks:
+            if block + 1 < blocks and not carried:
                 top = score(block + 1, x, query, query_clip, top)
             weights = jnp.exp2(s_ref[block % 2, :, x * OWN : (x + 1) * OWN] * factor - shift)
             for j in range(0, OWN, HEAD):
                 total = total + weights[:, j : j + HEAD]
+            if block + 1 < blocks and carried:
+                top = score(block + 1, x, query, query_clip, top)
             numerator = numerator + jnp.dot(
                 weights.astype(jnp.bfloat16), kv_ref[x, 1], preferred_element_type=jnp.float32
             )

time: 72.2 us -> 72.2 us (level)
  no operation moved by 1% of the time
where the time goes in v10:
time: 72.2 us; the launch traced here: 71.9 us
  blocking collectives  60.6 us (84%)
  Pallas kernels  5.11 us (7%)
  starting transfers between devices  3.9 us (5%)
  matrix products  1.38 us (2%)
  local copies, waits for them, and re-layouts  0.89 us (1%)
    all_to_all x3, blocking collectives, exchange(): lax.all_to_all(array, 'device', 0, 0, axis_index_groups=groups.tolist(),...  60.6 us
    pallas_call x2, Pallas kernels, attend(): pl.pallas_call(functools.partial(attend_kernel, its_core, bool(state)), o...  5.11 us
    ppermute x1, starting transfers between devices, body(): lax.ppermute(near, 'device', [(a, b) for a, b in BY_CORE.tolist()] + [(b,...  3.9 us
  transfers between devices with their start and end apart: 1, of which 0 were waited for; matrix products, arithmetic and copies ran while one was open for 0% of the time, Pallas kernels for 3%

profile of v10, /device:TPU:1, one launch (start us, length us, event | category | flops | bytes accessed | tf_op | source)
XLA Modules:
  0.0 71.9 jit_solution(2610998193590181259)
XLA Ops:
  0.0 1.4 %fusion.1 = bf16[3,64,8,128]{3,2,1,0:T(8,128)(2,1)S(1)} fusion(s32[8192]{0:T(1024)S(1)} %add_select_fusion, bf16[8,6144]{1,0:T(8,128)(2,1)} %param.7, bf16[8,6144]{1,0:T(8,128)(2,1)} %param.6, bf16[8,6144]{1,0:T(8,128)(2,1)} %param.5, s32[3,8,48]{2,1,0:T(8,128)} %param.8), kind=kOutput, calls=%fused_computation.3 | convolution fusion | flops 21826944 | bytes 725504 | tf_op jit(solution)/shard_map/dot_general | solution.py:138
  1.4 0.1 copy.11
  1.5 28.7 %all_to_all.15 = bf16[64,24,128]{2,1,0:T(8,128)(2,1)S(1)} all-to-all(bf16[64,24,128]{2,1,0:T(8,128)(2,1)S(1)} %bitcast.26), channel_id=1, replica_groups={{328,392,456,8,72,136,200,264,330,394,458,10,74,138,202,266,332,396,460..., dimensions={0} | all-to-all | bytes 786432 | tf_op jit(solution)/shard_map/all_to_all | solution.py:146
  30.2 0.1 concatenate.7
  30.3 0.0 copy-start
  30.3 16.3 %all_to_all.16.kv_ref = bf16[4,2,512,128]{3,2,1,0:T(8,128)(2,1)S(1)} all-to-all(bf16[4,2,512,128]{3,2,1,0:T(8,128)(2,1)S(1)} %concatenate.7), channel_id=1, replica_groups={{32,1,33,0},{34,3,35,2},{36,5,37,4},{38,7,39,6},{40,9,41,8},{42,11,43,1..., dimensions={0} | all-to-all | bytes 2097152 | tf_op jit(solution)/shard_map/all_to_all | solution.py:146
  46.6 3.9 %collective-permute-start = (bf16[4,2,512,128]{3,2,1,0:T(8,128)(2,1)S(1)}, bf16[4,2,512,128]{3,2,1,0:T(8,128)(2,1)S(1)}, u32[]{:S(2)}, u32[]{:S(2)}) collective-permute-start(bf16[4,2,512,128]{3,2,1,0:T(8,128)(2,1)S(1)} %all_to_all.16.kv_ref), channel_id=1, source_target_pairs={{0,16},{1,17},{2,18},{3,19},{4,20},{5,21},{6,22},{7,23},{8,24},{9,... | collective-permute-start | bytes 3145736 | tf_op jit(solution)/shard_map/ppermute | solution.py:156
  50.5 0.0 copy-done
  50.5 2.5 %shard_map.55 = (f32[512,128]{1,0:T(8,128)S(1)}, f32[512,128]{1,0:T(8,128)S(1)}, f32[512,128]{1,0:T(8,128)S(1)}) custom-call(s32[4]{0:T(128)S(1)} %copy-done, bf16[512,128]{1,0:T(8,128)(2,1)S(1)} %slice_bitcast_fusion.1.q_ref, bf16[4,2,512,128]{3,2,1,0:T(8,128)(2,1)S(1)} %all_to_all.16.kv_ref), custom_call_target="tpu_custom_call" | custom-call | flops 536870912 | bytes 1048576 | tf_op jit(solution)/shard_map/pallas_call | solution.py:121
  53.0 0.0 collective-permute-done.kv_ref
  53.0 2.7 %shard_map.56 = bf16[512,128]{1,0:T(8,128)(2,1)S(1)} custom-call(s32[4]{0:T(128)S(1)} %copy-done, bf16[512,128]{1,0:T(8,128)(2,1)S(1)} %slice_bitcast_fusion.1.q_ref, bf16[4,2,512,128]{3,2,1,0:T(8,128)(2,1)S(1)} %collective-permute-done.kv_ref, f32[512,128]{1,0:T(8,128)S(1)} %get-tuple-element.8.refs_0_, f32[512,128]{1,0:T(8,128)S(1)} %get-tuple-element.9.refs_1_, ...), custom_call_target="tpu_custom_call" | custom-call | flops 536870912 | bytes 1048576 | tf_op jit(solution)/shard_map/pallas_call | solution.py:121
  55.7 15.6 %all_to_all.17 = bf16[64,8,128]{2,1,0:T(8,128)(2,1)S(1)} all-to-all(bf16[64,8,128]{2,1,0:T(8,128)(2,1)S(1)} %bitcast.25), channel_id=1, replica_groups={{328,392,456,8,72,136,200,264,330,394,458,10,74,138,202,266,332,396,460..., dimensions={0} | all-to-all | bytes 262144 | tf_op jit(solution)/shard_map/all_to_all | solution.py:146
  71.3 0.6 slice_bitcast_fusion.2
  (3 shorter events, 0.0 us)
Async XLA Ops:
  30.3 20.2 %copy-start = (s32[4]{0:T(128)S(1)}, s32[4]{0:T(128)}, u32[]{:S(2)}) copy-start(s32[4]{0:T(128)} %length_ref.3) | copy-start | bytes 52
  46.6 6.4 %collective-permute-start = (bf16[4,2,512,128]{3,2,1,0:T(8,128)(2,1)S(1)}, bf16[4,2,512,128]{3,2,1,0:T(8,128)(2,1)S(1)}, u32[]{:S(2)}, u32[]{:S(2)}) collective-permute-start(bf16[4,2,512,128]{3,2,1,0:T(8,128)(2,1)S(1)} %all_to_all.16.kv_ref), channel_id=1, source_target_pairs={{0,16},{1,17},{2,18},{3,19},{4,20},{5,21},{6,22},{7,23},{8,24},{9,... | collective-permute-start | bytes 3145736 | tf_op jit(solution)/shard_map/ppermute | solution.py:156

commit v11 on v9

--- a/solution.py
+++ b/solution.py
@@ -16,7 +16,7 @@
 HEAD = 128
 ROWS = 8
 OWN = SLOTS * ROWS
-FIRST_Z, FIRST_Y = 5, 4
+FIRST_Z, FIRST_Y = 6, 4
 X_ORDER = [2, 1, 3, 0]
 PLACES = np.arange(512).reshape(SIZES)
 BY_HEAD = np.roll(PLACES, (-FIRST_Z, -FIRST_Y), (0, 3)).transpose(1, 2, 4, 3, 0).reshape(8, SLOTS)

time: 72.2 us -> 72.6 us (level)
  no operation moved by 1% of the time
where the time goes in v11:
time: 72.6 us; the launch traced here: 72.3 us
  blocking collectives  60.9 us (84%)
  Pallas kernels  5.11 us (7%)
  starting transfers between devices  3.9 us (5%)
  matrix products  1.38 us (2%)
  local copies, waits for them, and re-layouts  0.89 us (1%)
    all_to_all x3, blocking collectives, exchange(): lax.all_to_all(array, 'device', 0, 0, axis_index_groups=groups.tolist(),...  60.9 us
    pallas_call x2, Pallas kernels, attend(): pl.pallas_call(functools.partial(attend_kernel, its_core, bool(state)), o...  5.11 us
    ppermute x1, starting transfers between devices, body(): lax.ppermute(near, 'device', [(a, b) for a, b in BY_CORE.tolist()] + [(b,...  3.9 us
  transfers between devices with their start and end apart: 1, of which 0 were waited for; matrix products, arithmetic and copies ran while one was open for 0% of the time, Pallas kernels for 3%

profile of v11, /device:TPU:1, one launch (start us, length us, event | category | flops | bytes accessed | tf_op | source)
XLA Modules:
  0.0 72.3 jit_solution(10435124204916499175)
XLA Ops:
  0.0 1.4 %fusion.1 = bf16[3,64,8,128]{3,2,1,0:T(8,128)(2,1)S(1)} fusion(s32[8192]{0:T(1024)S(1)} %add_select_fusion, bf16[8,6144]{1,0:T(8,128)(2,1)} %param.7, bf16[8,6144]{1,0:T(8,128)(2,1)} %param.6, bf16[8,6144]{1,0:T(8,128)(2,1)} %param.5, s32[3,8,48]{2,1,0:T(8,128)} %param.8), kind=kOutput, calls=%fused_computation.3 | convolution fusion | flops 21826944 | bytes 725504 | tf_op jit(solution)/shard_map/dot_general | solution.py:136
  1.4 0.1 copy.11
  1.5 28.8 %all_to_all.15 = bf16[64,24,128]{2,1,0:T(8,128)(2,1)S(1)} all-to-all(bf16[64,24,128]{2,1,0:T(8,128)(2,1)S(1)} %bitcast.26), channel_id=1, replica_groups={{392,456,8,72,136,200,264,328,394,458,10,74,138,202,266,330,396,460,12,..., dimensions={0} | all-to-all | bytes 786432 | tf_op jit(solution)/shard_map/all_to_all | solution.py:144
  30.3 0.1 concatenate.7
  30.5 0.0 copy-start
  30.5 16.3 %all_to_all.16.kv_ref = bf16[4,2,512,128]{3,2,1,0:T(8,128)(2,1)S(1)} all-to-all(bf16[4,2,512,128]{3,2,1,0:T(8,128)(2,1)S(1)} %concatenate.7), channel_id=1, replica_groups={{32,1,33,0},{34,3,35,2},{36,5,37,4},{38,7,39,6},{40,9,41,8},{42,11,43,1..., dimensions={0} | all-to-all | bytes 2097152 | tf_op jit(solution)/shard_map/all_to_all | solution.py:144
  46.7 3.9 %collective-permute-start = (bf16[4,2,512,128]{3,2,1,0:T(8,128)(2,1)S(1)}, bf16[4,2,512,128]{3,2,1,0:T(8,128)(2,1)S(1)}, u32[]{:S(2)}, u32[]{:S(2)}) collective-permute-start(bf16[4,2,512,128]{3,2,1,0:T(8,128)(2,1)S(1)} %all_to_all.16.kv_ref), channel_id=1, source_target_pairs={{0,16},{1,17},{2,18},{3,19},{4,20},{5,21},{6,22},{7,23},{8,24},{9,... | collective-permute-start | bytes 3145736 | tf_op jit(solution)/shard_map/ppermute | solution.py:154
  50.7 0.0 copy-done
  50.7 2.5 %shard_map.55 = (f32[512,128]{1,0:T(8,128)S(1)}, f32[512,128]{1,0:T(8,128)S(1)}, f32[512,128]{1,0:T(8,128)S(1)}) custom-call(s32[4]{0:T(128)S(1)} %copy-done, bf16[512,128]{1,0:T(8,128)(2,1)S(1)} %slice_bitcast_fusion.1.q_ref, bf16[4,2,512,128]{3,2,1,0:T(8,128)(2,1)S(1)} %all_to_all.16.kv_ref), custom_call_target="tpu_custom_call" | custom-call | flops 536870912 | bytes 1048576 | tf_op jit(solution)/shard_map/pallas_call | solution.py:119
  53.1 0.0 collective-permute-done.kv_ref
  53.1 2.7 %shard_map.56 = bf16[512,128]{1,0:T(8,128)(2,1)S(1)} custom-call(s32[4]{0:T(128)S(1)} %copy-done, bf16[512,128]{1,0:T(8,128)(2,1)S(1)} %slice_bitcast_fusion.1.q_ref, bf16[4,2,512,128]{3,2,1,0:T(8,128)(2,1)S(1)} %collective-permute-done.kv_ref, f32[512,128]{1,0:T(8,128)S(1)} %get-tuple-element.8.refs_0_, f32[512,128]{1,0:T(8,128)S(1)} %get-tuple-element.9.refs_1_, ...), custom_call_target="tpu_custom_call" | custom-call | flops 536870912 | bytes 1048576 | tf_op jit(solution)/shard_map/pallas_call | solution.py:119
  55.8 15.9 %all_to_all.17 = bf16[64,8,128]{2,1,0:T(8,128)(2,1)S(1)} all-to-all(bf16[64,8,128]{2,1,0:T(8,128)(2,1)S(1)} %bitcast.25), channel_id=1, replica_groups={{392,456,8,72,136,200,264,328,394,458,10,74,138,202,266,330,396,460,12,..., dimensions={0} | all-to-all | bytes 262144 | tf_op jit(solution)/shard_map/all_to_all | solution.py:144
  71.7 0.6 slice_bitcast_fusion.2
  (3 shorter events, 0.0 us)
Async XLA Ops:
  30.5 20.2 %copy-start = (s32[4]{0:T(128)S(1)}, s32[4]{0:T(128)}, u32[]{:S(2)}) copy-start(s32[4]{0:T(128)} %length_ref.3) | copy-start | bytes 52
  46.7 6.4 %collective-permute-start = (bf16[4,2,512,128]{3,2,1,0:T(8,128)(2,1)S(1)}, bf16[4,2,512,128]{3,2,1,0:T(8,128)(2,1)S(1)}, u32[]{:S(2)}, u32[]{:S(2)}) collective-permute-start(bf16[4,2,512,128]{3,2,1,0:T(8,128)(2,1)S(1)} %all_to_all.16.kv_ref), channel_id=1, source_target_pairs={{0,16},{1,17},{2,18},{3,19},{4,20},{5,21},{6,22},{7,23},{8,24},{9,... | collective-permute-start | bytes 3145736 | tf_op jit(solution)/shard_map/ppermute | solution.py:154
